TPU v7x, 256 devices: a whole 4x4x8 slice. The times are simulated.
256 devices in a mesh: dp: 8 (over z_lo, x), ctx: 32 (over y, z_hi, core).
Axes of the slice: x: 4, y: 4, z: 8 (z_hi: 4, z_lo: 2; z = z_hi * 2 + z_lo), core: 2. Of those that a mesh axis runs over, the one named last changes fastest.
Arguments:
- vit_states: bfloat16 [8, 4096, 2560], P('dp', 'ctx')
- norm_gain: float32 [640], replicated, may hold values from 0.5 to 1.5
- w_first: bfloat16 [2560, 2560], P('dp'), may hold values from -0.125 to 0.125
- b_first: float32 [2560], P('dp'), may hold values from -3 to 3
- w_second: bfloat16 [2560, 4096], P('dp'), may hold values from -0.125 to 0.125
- llm_grad: bfloat16 [8, 4096, 4096], P('dp', 'ctx'), may hold values from -6 to 6
- block_order: int32 [64], replicated, may hold values from 0 to 63, as said below
- frame_tokens: int32 [8, 128], replicated, may hold values from 8 to 32, as said below
Outputs:
- vit_grad: bfloat16 [8, 4096, 2560], P('dp', 'ctx')
- w_first_grad: float32 [2560, 2560], P('dp', 'ctx')
- w_second_grad: float32 [2560, 4096], P('dp', 'ctx')
Inputs may be any that keep to these rules, and one draw needn't show every extreme that they name: `block_order`: a permutation of 0 to 63 in which entries 2 c and 2 c + 1 add up to 63 for every c. `frame_tokens`: every video has a frame with all 32 slots used.
All inputs are finite; a program needn't handle non-finite values.
Results may differ from a plain program's by a relative error of at most 0.02.
Values may be sent and summed in bfloat16 or wider, within the bound.
A program may use at most 128 MiB of HBM per device.

v0:
```python
import math

import jax
import jax.numpy as jnp
from jax import lax
from jax.sharding import PartitionSpec as P

FRAME_SLOTS = 32


epsilon = 1e-06


def gelu_value(values):
    return 0.5 * values * (1.0 + jax.scipy.special.erf(values * (1.0 / math.sqrt(2.0))))


def gelu_slope(values):
    normal_cdf = 0.5 * (1.0 + jax.scipy.special.erf(values * (1.0 / math.sqrt(2.0))))
    density = jnp.exp(-0.5 * values * values) * (1.0 / math.sqrt(2.0 * math.pi))
    return normal_cdf + values * density


def body(vit_states, norm_gain, w_first, b_first, w_second, llm_grad, block_order, frame_tokens):
    own_rows = vit_states.shape[1]
    width_in = vit_states.shape[2]
    width_llm = llm_grad.shape[2]
    features = norm_gain.shape[0]
    shards = lax.axis_size("ctx")
    groups = lax.axis_size("dp")
    all_rows = own_rows * shards
    blocks = 2 * shards
    block_rows = own_rows // 2
    positions = jnp.arange(blocks, dtype=jnp.int32)
    matches = (block_order[None, :] == positions[:, None]).astype(jnp.int32)
    inverse = jnp.sum(matches * positions[None, :], axis=1)
    states = vit_states[0].astype(jnp.float32).reshape(own_rows, 4, features)
    inv_rms = lax.rsqrt(jnp.mean(states * states, axis=-1, keepdims=True) + epsilon)
    scaled = states * inv_rms
    normed = (scaled * norm_gain).astype(jnp.bfloat16).reshape(own_rows, width_in)
    llm_rows, input_rows = (
        lax.all_gather(llm_grad[0], "dp", axis=0, tiled=True),
        lax.all_gather(normed, "dp", axis=0, tiled=True),
    )
    stacked = llm_rows.reshape(groups, own_rows, width_llm)
    spread = lax.all_to_all(stacked, "ctx", split_axis=2, concat_axis=1, tiled=True)
    ordered = jnp.take(spread.reshape(groups, blocks, block_rows, -1), inverse, axis=1).reshape(
        groups, all_rows, -1
    )
    back = lax.all_to_all(ordered, "ctx", split_axis=1, concat_axis=2, tiled=True)
    grad_rows = back.reshape(groups * own_rows, width_llm)
    slot_ids = jnp.arange(FRAME_SLOTS, dtype=jnp.int32)
    keep_all = (slot_ids[None, None, :] < frame_tokens[:, :, None]).reshape(groups, all_rows)
    keep_own = lax.dynamic_slice_in_dim(
        keep_all, lax.axis_index("ctx") * own_rows, own_rows, 1
    ).reshape(groups * own_rows)
    masked = jnp.where(keep_own[:, None], grad_rows, jnp.zeros_like(grad_rows))
    contract_cols = (((1,), (1,)), ((), ()))
    contract_rows = (((0,), (0,)), ((), ()))
    pre_act = (
        lax.dot_general(input_rows, w_first, contract_cols, preferred_element_type=jnp.float32)
        + b_first[None, :]
    )
    activated = gelu_value(pre_act).astype(jnp.bfloat16)
    hidden_grad = lax.dot_general(
        masked, w_second, contract_cols, preferred_element_type=jnp.float32
    )
    pre_grad = (hidden_grad * gelu_slope(pre_act)).astype(jnp.bfloat16)
    second_local = lax.dot_general(
        activated, masked, contract_rows, preferred_element_type=jnp.float32
    )
    first_local = lax.dot_general(
        pre_grad, input_rows, contract_rows, preferred_element_type=jnp.float32
    )
    first_grad, second_grad = (
        lax.psum_scatter(
            first_local.astype(jnp.bfloat16), "ctx", scatter_dimension=1, tiled=True
        ).astype(jnp.float32),
        lax.psum_scatter(
            second_local.astype(jnp.bfloat16), "ctx", scatter_dimension=1, tiled=True
        ).astype(jnp.float32),
    )
    normed_grad = lax.psum_scatter(
        jnp.dot(pre_grad, w_first, preferred_element_type=jnp.float32).astype(jnp.bfloat16),
        "dp",
        scatter_dimension=0,
        tiled=True,
    ).astype(jnp.float32)
    scaled_grad = normed_grad.reshape(own_rows, 4, features) * norm_gain
    vit_rows = inv_rms * (
        scaled_grad - scaled * jnp.mean(scaled_grad * scaled, axis=-1, keepdims=True)
    )
    vit_grad = vit_rows.astype(jnp.bfloat16).reshape(1, own_rows, width_in)
    return (vit_grad, first_grad, second_grad)


def solution(mesh):
    placed = (
        P("dp", "ctx", None),
        P(),
        P("dp", None),
        P("dp"),
        P("dp", None),
        P("dp", "ctx", None),
        P(),
        P(),
    )
    return jax.shard_map(
        body,
        mesh=mesh,
        in_specs=placed,
        out_specs=(P("dp", "ctx", None), P("dp", "ctx"), P("dp", "ctx")),
        check_vma=False,
    )
```

profile of v0, /device:TPU:1, one launch (start us, length us, event | category | flops | bytes accessed | tf_op | source)
XLA Modules:
  0.0 901.4 jit_solution(9179358867517933409)
XLA Ops:
  7.2 0.0 copy-start
  7.2 0.0 all-gather.6.cloned.1.call-start
  7.2 0.7 all-gather.6.cloned.1.call-update
  7.9 100.2 %all-gather.6.cloned.1.call-done = bf16[1,1024,4096]{2,1,0:T(8,128)(2,1)} async-done(((bf16[1,128,4096]{2,1,0:T(8,128)(2,1)}), bf16[1,1024,4096]{2,1,0:T(8,128)(2,1)}) %all-gather.6.cloned.1.call-update) | async-done | bytes 8388624 | tf_op jit(solution)/shard_map/all_gather | solution.py:42
  108.1 12.0 %copy.25 = bf16[8,128,4096]{1,0,2:T(8,128)(2,1)} copy(bf16[8,128,4096]{2,1,0:T(8,128)(2,1)} %bitcast.56) | data formatting | bytes 16777216 | tf_op jit(solution)/shard_map/reshape | solution.py:45
  120.1 9.6 %all-to-all-start = ((bf16[8,128,4096]{1,0,2:T(8,128)(2,1)}), bf16[8,128,4096]{1,0,2:T(8,128)(2,1)}, u32[]{:S(2)}, u32[]{:S(2)}) async-start(bf16[8,128,4096]{1,0,2:T(8,128)(2,1)} %copy.25), calls=%async_computation | async-start | bytes 16777216 | tf_op jit(solution)/shard_map/all_to_all | solution.py:46
  129.7 0.0 copy-done.6
  129.7 0.1 select_reduce_fusion
  129.8 0.1 broadcast_in_dim.39
  129.9 0.1 broadcast_in_dim.40
  130.0 148.9 %all-to-all-done = bf16[8,128,4096]{1,0,2:T(8,128)(2,1)} async-done(((bf16[8,128,4096]{1,0,2:T(8,128)(2,1)}), bf16[8,128,4096]{1,0,2:T(8,128)(2,1)}, u32[]{:S(2)}, u32[]{:S(2)}) %all-to-all-start) | async-done | bytes 8388640 | tf_op jit(solution)/shard_map/all_to_all | solution.py:46
  279.0 12.2 %copy.27 = bf16[8,32,128,128]{3,2,1,0:T(8,128)(2,1)} copy(bf16[8,32,128,128]{2,0,3,1:T(8,128)(2,1)} %bitcast.4) | data formatting | bytes 16777216 | tf_op jit(solution)/shard_map/all_to_all | solution.py:46
  291.2 8.9 gather_fusion
  300.1 9.5 %copy.28 = bf16[8,64,64,128]{3,2,1,0:T(8,128)(2,1)} copy(bf16[8,64,64,128]{3,2,0,1:T(8,128)(2,1)} %bitcast.51) | data formatting | bytes 16777216 | tf_op jit(solution)/shard_map/jit(_take)/gather | solution.py:47
  309.6 4.5 bitcast_select_fusion.1
  314.2 25.1 %copy.29 = bf16[8,4096,128]{2,0,1:T(8,128)(2,1)} copy(bf16[8,4096,128]{2,1,0:T(8,128)(2,1)S(1)} %bitcast_select_fusion.1) | data formatting | bytes 16777216 | tf_op jit(solution)/shard_map/jit(_take)/select_n | solution.py:47
  339.3 23.6 %all-to-all-start.1 = ((bf16[8,4096,128]{2,0,1:T(8,128)(2,1)}), bf16[8,4096,128]{2,0,1:T(8,128)(2,1)}, u32[]{:S(2)}, u32[]{:S(2)}) async-start(bf16[8,4096,128]{2,0,1:T(8,128)(2,1)} %copy.29), calls=%async_computation.1 | async-start | bytes 16777216 | tf_op jit(solution)/shard_map/all_to_all | solution.py:50
  362.9 0.0 all-gather.4.cloned.1.call-start
  363.0 0.0 copy-done.3
  363.0 0.0 copy-done.2
  363.0 1.5 reshape.88
  364.5 1.6 multiply_reduce_fusion.1
  366.2 0.2 mul.119
  366.5 0.0 copy-start.1
  366.5 0.1 copy.37
  366.6 1.0 copy-done.1
  367.5 1.0 fusion.10
  368.6 0.0 all-gather.4.cloned.1.call-update
  368.6 0.0 reduce-scatter.8.cloned.1.call-start
  368.6 0.1 lt.45
  368.7 0.0 copy-done.4
  368.7 1.0 lt.47
  369.8 1.3 lt.48
  371.0 0.1 dynamic-slice
  371.1 199.5 %all-gather.4.cloned.1.call-done = bf16[1024,2560]{1,0:T(8,128)(2,1)} async-done(((bf16[128,2560]{1,0:T(8,128)(2,1)}), bf16[1024,2560]{1,0:T(8,128)(2,1)}) %all-gather.4.cloned.1.call-update) | async-done | bytes 5242896 | tf_op jit(solution)/shard_map/all_gather | solution.py:43
  570.6 0.0 copy-done.5
  570.6 6.0 convolution_add_fusion
  576.6 22.6 %all-to-all-done.1 = bf16[8,4096,128]{2,0,1:T(8,128)(2,1)} async-done(((bf16[8,4096,128]{2,0,1:T(8,128)(2,1)}), bf16[8,4096,128]{2,0,1:T(8,128)(2,1)}, u32[]{:S(2)}, u32[]{:S(2)}) %all-to-all-start.1) | async-done | bytes 8388640 | tf_op jit(solution)/shard_map/all_to_all | solution.py:50
  599.3 12.2 %copy.31 = bf16[8,128,32,128]{3,2,1,0:T(8,128)(2,1)} copy(bf16[8,128,32,128]{3,0,1,2:T(8,128)(2,1)} %bitcast.12) | data formatting | bytes 16777216 | tf_op jit(solution)/shard_map/all_to_all | solution.py:50
  611.4 9.4 %fusion.2 = bf16[1024,320]{0,1:T(8,128)(2,1)S(1)} fusion(bf16[320,4096]{1,0:T(8,128)(2,1)S(1)} %copy-done, bf16[128,8,32,128]{3,2,1,0:T(8,128)(2,1)} %bitcast.54, pred[1024]{0:T(1024)(128)(4,1)S(1)} %fusion.12, f32[1024,320]{0,1:T(8,128)S(1)} %copy-done.8), kind=kOutput, calls=%fused_computation.10 | convolution fusion | flops 2691825664 | bytes 12977152 | tf_op jit(solution)/shard_map/dot_general | solution.py:65
  620.8 0.0 copy-start.7
  620.8 0.8 copy-done.7
  621.7 0.0 slice-done.1
  621.7 4.3 convolution_convert_fusion.2
  625.9 0.0 reduce-scatter.8.cloned.1.call-update
  625.9 0.0 reduce-scatter.10.cloned.1.call-start
  626.0 8.9 convolution_convert_fusion.1
  634.9 4.6 copy.34
  639.6 0.0 reduce-scatter.10.cloned.1.call-update
  639.6 0.0 reduce-scatter.6.cloned.1.call-start
  639.6 6.9 convolution_convert_fusion
  646.5 0.0 reduce-scatter.6.cloned.1.call-update
  646.6 3.0 mul.120
  649.6 68.4 %reduce-scatter.8.cloned.1.call-done = bf16[320,80]{0,1:T(8,128)(2,1)} async-done(((bf16[320,2560]{0,1:T(8,128)(2,1)}), bf16[320,80]{0,1:T(8,128)(2,1)}) %reduce-scatter.8.cloned.1.call-update) | async-done | bytes 51216 | tf_op jit(solution)/shard_map/reduce_scatter | solution.py:76
  718.0 1.5 convert_element_type.64
  719.5 96.0 %reduce-scatter.10.cloned.1.call-done = bf16[128,320]{1,0:T(8,128)(2,1)} async-done(((bf16[4096,320]{1,0:T(8,128)(2,1)}), bf16[128,320]{1,0:T(8,128)(2,1)}) %reduce-scatter.10.cloned.1.call-update) | async-done | bytes 81936
  815.5 1.0 copy.35
  816.5 0.7 convert_element_type.67
  817.2 65.7 %reduce-scatter.6.cloned.1.call-done = bf16[128,2560]{1,0:T(8,128)(2,1)} async-done(((bf16[1024,2560]{1,0:T(8,128)(2,1)}), bf16[128,2560]{1,0:T(8,128)(2,1)}) %reduce-scatter.6.cloned.1.call-update) | async-done | bytes 655376 | tf_op jit(solution)/shard_map/reduce_scatter | solution.py:83
  882.9 2.6 reshape.87
  885.5 2.4 multiply_reduce_fusion
  887.8 1.3 mul.146
  889.1 2.7 mul.147
  891.9 3.0 fusion.8
  (21 shorter events, 0.1 us)
Async XLA Ops:
  7.2 604.3 %copy-start = (bf16[320,4096]{1,0:T(8,128)(2,1)S(1)}, bf16[320,4096]{1,0:T(8,128)(2,1)}, u32[]{:S(2)}) copy-start(bf16[320,4096]{1,0:T(8,128)(2,1)} %param.12) | copy-start | bytes 7864324
  7.2 101.0 %all-gather.6.cloned.1.call-start = ((), (), s32[]{:S(2)}) async-start(), calls=%async_computation.8 | async-start | bytes 9437184 | tf_op jit(solution)/shard_map/all_gather | solution.py:42
  120.1 9.6 %copy-start.6 = (s32[64]{0:T(128)S(1)}, s32[64]{0:T(128)}, u32[]{:S(2)}) copy-start(s32[64]{0:T(128)} %param.14) | copy-start | bytes 772
  120.1 158.9 %all-to-all-start = ((bf16[8,128,4096]{1,0,2:T(8,128)(2,1)}), bf16[8,128,4096]{1,0,2:T(8,128)(2,1)}, u32[]{:S(2)}, u32[]{:S(2)}) async-start(bf16[8,128,4096]{1,0,2:T(8,128)(2,1)} %copy.25), calls=%async_computation | async-start | bytes 16777216 | tf_op jit(solution)/shard_map/all_to_all | solution.py:46
  339.3 23.7 %copy-start.3 = (f32[640]{0:T(1024)S(1)}, f32[640]{0:T(1024)}, u32[]{:S(2)}) copy-start(f32[640]{0:T(1024)} %param.9) | copy-start | bytes 7684
  339.3 23.7 %copy-start.2 = (bf16[1,128,2560]{2,1,0:T(8,128)(2,1)S(1)}, bf16[1,128,2560]{2,1,0:T(8,128)(2,1)}, u32[]{:S(2)}) copy-start(bf16[1,128,2560]{2,1,0:T(8,128)(2,1)} %param.8) | copy-start | bytes 1966084
  339.3 260.0 %all-to-all-start.1 = ((bf16[8,4096,128]{2,0,1:T(8,128)(2,1)}), bf16[8,4096,128]{2,0,1:T(8,128)(2,1)}, u32[]{:S(2)}, u32[]{:S(2)}) async-start(bf16[8,4096,128]{2,0,1:T(8,128)(2,1)} %copy.29), calls=%async_computation.1 | async-start | bytes 16777216 | tf_op jit(solution)/shard_map/all_to_all | solution.py:50
  362.9 207.7 %all-gather.4.cloned.1.call-start = ((), (), s32[]{:S(2)}) async-start(), calls=%async_computation.5 | async-start | bytes 5898240 | tf_op jit(solution)/shard_map/all_gather | solution.py:43
  366.5 1.1 copy-start.1
  367.5 1.2 copy-start.4
  368.5 202.1 %copy-start.5 = (f32[320]{0:T(512)S(1)}, f32[320]{0:T(512)}, u32[]{:S(2)}) copy-start(f32[320]{0:T(512)} %param.11) | copy-start | bytes 3844
  368.6 349.4 %reduce-scatter.8.cloned.1.call-start = ((), (), s32[]{:S(2)}) async-start(), calls=%async_computation.7 | async-start | bytes 2027520 | tf_op jit(solution)/shard_map/reduce_scatter | solution.py:76
  599.3 12.2 %copy-start.8 = (f32[1024,320]{0,1:T(8,128)S(1)}, f32[1024,320]{0,1:T(8,128)}, u32[]{:S(2)}) copy-start(f32[1024,320]{0,1:T(8,128)} %convolution_add_fusion) | copy-start | bytes 3932164
  599.3 22.4 %slice-start = ((s8[5242880]{0:T(1024)(128)(4,1)}), s8[1048576]{0:T(1024)(128)(4,1)S(1)}, s32[]{:S(2)}) async-start(s8[5242880]{0:T(1024)(128)(4,1)} %bitcast.59), calls=%async_computation.10 | async-start | bytes 2097152
  611.4 10.2 %slice-start.1 = ((s8[5242880]{0:T(1024)(128)(4,1)}), s8[4194304]{0:T(1024)(128)(4,1)S(1)}, s32[]{:S(2)}) async-start(s8[5242880]{0:T(1024)(128)(4,1)} %bitcast.59), calls=%async_computation.11 | async-start | bytes 8388608
  620.8 0.8 copy-start.7
  625.9 189.6 %reduce-scatter.10.cloned.1.call-start = ((), (), s32[]{:S(2)}) async-start(), calls=%async_computation.9 | async-start | bytes 3244032
  639.6 243.3 %reduce-scatter.6.cloned.1.call-start = ((), (), s32[]{:S(2)}) async-start(), calls=%async_computation.6 | async-start | bytes 5898240 | tf_op jit(solution)/shard_map/reduce_scatter | solution.py:83
Sparse Core Ops, SparseCore 0:
  9.8 98.2 all-gather.5
  368.7 201.8 all-gather.3
  626.1 91.8 reduce-scatter.7
  722.3 93.1 reduce-scatter.9
  817.9 64.9 reduce-scatter.5
where the time goes:
time: 903 us; the launch traced here: 901 us
  waiting for transfers between devices  702 us (78%)
  local copies, waits for them, and re-layouts  102 us (11%)
  matrix products  35.5 us (4%)
  starting transfers between devices  33.4 us (4%)
  other arithmetic  14.9 us (2%)
  between operations  14 us (2%)
    all_gather x1, waiting for transfers between devices, body(): lax.all_gather(normed, 'dp', axis=0, tiled=True)  199 us
    all_to_all x1, waiting for transfers between devices, body(): lax.all_to_all(stacked, 'ctx', split_axis=2, concat_axis=1, tiled=True)  149 us
    all_gather x1, waiting for transfers between devices, body(): lax.all_gather(llm_grad[0], 'dp', axis=0, tiled=True)  100 us
    unnamed x6, waiting for transfers between devices  96.7 us
    reduce_scatter x1, waiting for transfers between devices, body(): lax.psum_scatter(first_local.astype(jnp.bfloat16), 'ctx', scatter_dimensi...  68.4 us
    reduce_scatter x1, waiting for transfers between devices, body(): lax.psum_scatter(jnp.dot(pre_grad, w_first, preferred_element_type=jnp.fl...  65.7 us
    select_n x1, local copies, waits for them, and re-layouts, body(): jnp.take(spread.reshape(groups, blocks, block_rows, -1), inverse, axis=1)  25.1 us
    all_to_all x1, starting transfers between devices, body(): lax.all_to_all(ordered, 'ctx', split_axis=1, concat_axis=2, tiled=True)  23.6 us
  transfers between devices with their start and end apart: 7, of which 7 were waited for; matrix products, arithmetic and copies ran while one was open for 4% of the time, Pallas kernels for 0%

commit v1 on v0

v1 whole, which is shorter than its diff:
```python
import functools
import math

import jax
import jax.numpy as jnp
from jax import lax
from jax.experimental import pallas as pl
from jax.experimental.pallas import tpu as pltpu
from jax.sharding import PartitionSpec as P

MESH = pl.DeviceIdType.MESH
EPS = 1e-06
X, Y, Z, CTX = 4, 4, 8, 32
ROWS = 128
SEG = 640
F32, BF16 = jnp.float32, jnp.bfloat16


def gelu_value(values):
    return 0.5 * values * (1.0 + lax.erf(values * (1.0 / math.sqrt(2.0))))


def gelu_slope(values):
    normal_cdf = 0.5 * (1.0 + lax.erf(values * (1.0 / math.sqrt(2.0))))
    density = jnp.exp(-0.5 * values * values) * (1.0 / math.sqrt(2.0 * math.pi))
    return normal_cdf + values * density


def place():
    dp, ctx = lax.axis_index("dp"), lax.axis_index("ctx")
    x, y, core = lax.rem(dp, X), ctx // 8, lax.rem(ctx, 2)
    z = lax.rem(ctx // 2, 4) * 2 + dp // X
    return x, y, z, core


def device(x, y, z, core):
    return (lax.rem(z, 2) * X + x, y * 8 + (z // 2) * 2 + core)


def greet(others):
    barrier = pltpu.get_barrier_semaphore()
    for other in others:
        pl.semaphore_signal(barrier, inc=1, device_id=other, device_id_type=MESH)
    return barrier


def remote(src, dst, send, recv, to):
    return pltpu.make_async_remote_copy(
        src_ref=src, dst_ref=dst, send_sem=send, recv_sem=recv, device_id=to, device_id_type=MESH
    )


def loop(n, body):
    lax.fori_loop(0, n, lambda i, c: (body(i), c)[1], 0)


def gather_kernel(
    inv, order, frames, llm, vit, gain, bias, w1, w2,
    llm_rows, n_rows, w1_all, w2_all, b_all,
    masked, normed, recv1, send2,
    s1, r1, s2, r2, loc, wsend, wrecv, nsend, nrecv, lsend, lrecv,
):
    x, y, z, core = place()
    ctx, dp = lax.axis_index("ctx"), lax.axis_index("dp")
    right, left = lax.rem(x + 1, X), lax.rem(x + X - 1, X)
    to_right, to_left = device(right, y, z, core), device(left, y, z, core)
    up, down = lax.rem(z + 1, Z), lax.rem(z + Z - 1, Z)
    z_to = jnp.where(core == 0, up, down)
    z_from = jnp.where(core == 0, down, up)
    to_z, from_z = device(x, y, z_to, core), device(x, y, z_from, core)
    sibling = device(x, y, z, 1 - core)

    barrier = greet([to_right, to_left, to_z, from_z])

    def hello(k):
        pl.semaphore_signal(
            barrier, inc=1, device_id=(dp, lax.rem(ctx + k + 1, CTX)), device_id_type=MESH
        )

    loop(CTX - 1, hello)

    for block in range(2):
        t = order[2 * ctx + block]
        for frame in range(2):
            count = frames[dp, 2 * t + frame]
            keep = lax.broadcasted_iota(jnp.int32, (32, 512), 0) < count

            def mask(c):
                at = (block, pl.ds(32 * frame, 32), pl.ds(pl.multiple_of(c * 512, 512), 512))
                masked[at] = jnp.where(keep, llm[at].astype(F32), 0.0).astype(BF16)

            loop(8, mask)

    pl.semaphore_wait(barrier, CTX - 1 + 4)

    def cols(i):
        return pl.ds(pl.multiple_of(i * 128, 128), 128)

    def first(k):
        t = lax.rem(ctx + k + 1, CTX)
        return remote(masked.at[:, :, cols(t)], recv1.at[ctx], s1.at[k], r1.at[ctx], (dp, t))

    loop(CTX - 1, lambda k: first(k).start())
    own1 = pltpu.make_async_copy(masked.at[:, :, cols(ctx)], recv1.at[ctx], loc.at[0])
    own1.start()

    def norm(i):
        rows = pl.ds(pl.multiple_of(i * 32, 32), 32)
        for seg in range(4):
            at = (rows, slice(seg * SEG, (seg + 1) * SEG))
            states = vit[at].astype(F32)
            inv_rms = lax.rsqrt(jnp.mean(states * states, axis=-1, keepdims=True) + EPS)
            normed[i // 2, pl.ds(pl.multiple_of(lax.rem(i, 2) * 32, 32), 32), at[1]] = (
                states * inv_rms * gain[...]
            ).astype(BF16)

    loop(4, norm)

    def spread(rows, own, send, recv, which):
        here = pltpu.make_async_copy(own, rows.at[x], loc.at[which])
        a = remote(own, rows.at[x], send.at[0], recv.at[0], to_right)
        b = remote(own, rows.at[x], send.at[1], recv.at[1], to_left)
        return here, a, b

    def forward(rows, send, recv):
        c = remote(rows.at[left, 0], rows.at[left, 0], send.at[2], recv.at[2], to_right)
        d = remote(rows.at[right, 1], rows.at[right, 1], send.at[3], recv.at[3], to_left)
        return c, d

    n_here, n_a, n_b = spread(n_rows, normed, nsend, nrecv, 1)
    for c in (n_here, n_a, n_b):
        c.start()

    keep_w = [
        pltpu.make_async_copy(src, dst.at[0], loc.at[2 + i])
        for i, (src, dst) in enumerate(((w1, w1_all), (w2, w2_all), (bias, b_all)))
    ]
    for c in keep_w:
        c.start()

    def first_here(k):
        s = lax.rem(ctx + k + 1, CTX)
        remote(masked.at[:, :, cols(0)], recv1.at[s], s1.at[k], r1.at[s], (dp, s)).wait_recv()

    loop(CTX - 1, first_here)
    own1.wait()

    def pick(d):
        for i in range(2):
            b = inv[2 * d + i]
            send2[d, i] = recv1[b // 2, lax.rem(b, 2)]

    def second(k):
        d = lax.rem(ctx + k + 1, CTX)
        return remote(
            send2.at[d], llm_rows.at[x, :, :, cols(ctx)], s2.at[k], r2.at[ctx], (dp, d)
        )

    def send_second(k):
        pick(lax.rem(ctx + k + 1, CTX))
        second(k).start()

    loop(CTX - 1, send_second)
    pick(ctx)
    own2 = pltpu.make_async_copy(send2.at[ctx], llm_rows.at[x, :, :, cols(ctx)], loc.at[5])
    own2.start()

    mine = pl.ds(pl.multiple_of(core * 160, 32), 160)
    theirs = pl.ds(pl.multiple_of((1 - core) * 160, 32), 160)
    w_copies = [
        remote(w1.at[mine], w1_all.at[1, mine], wsend.at[0], wrecv.at[0], to_z),
        remote(w2.at[mine], w2_all.at[1, mine], wsend.at[1], wrecv.at[1], to_z),
        remote(bias, b_all.at[1], wsend.at[2], wrecv.at[2], to_z),
    ]
    for c in w_copies:
        c.start()

    n_a.wait_recv()
    n_b.wait_recv()
    n_c, n_d = forward(n_rows, nsend, nrecv)
    n_c.start()
    n_d.start()

    def second_here(k):
        s = lax.rem(ctx + k + 1, CTX)
        remote(
            send2.at[0], llm_rows.at[x, :, :, cols(s)], s2.at[k], r2.at[s], (dp, s)
        ).wait_recv()

    loop(CTX - 1, second_here)
    own2.wait()

    l_a = remote(llm_rows.at[x], llm_rows.at[x], lsend.at[0], lrecv.at[0], to_right)
    l_b = remote(llm_rows.at[x], llm_rows.at[x], lsend.at[1], lrecv.at[1], to_left)
    l_a.start()
    l_b.start()

    for c in w_copies:
        c.wait_recv()
    w_shares = [
        remote(w1_all.at[1, mine], w1_all.at[1, mine], wsend.at[3], wrecv.at[3], sibling),
        remote(w2_all.at[1, mine], w2_all.at[1, mine], wsend.at[4], wrecv.at[4], sibling),
    ]
    for c in w_shares:
        c.start()

    l_a.wait_recv()
    l_b.wait_recv()
    l_c, l_d = forward(llm_rows, lsend, lrecv)
    l_c.start()
    l_d.start()

    for c in w_shares:
        c.wait_recv()
    n_c.wait_recv()
    n_d.wait_recv()
    l_c.wait_recv()
    l_d.wait_recv()
    n_here.wait()
    for c in keep_w:
        c.wait()
    for c in [n_a, n_b, n_c, n_d, l_a, l_b, l_c, l_d] + w_copies + w_shares:
        c.wait_send()

    def sent(k):
        first(k).wait_send()
        second(k).wait_send()

    loop(CTX - 1, sent)


def gather_rows(inv, order, frames, llm, vit, gain, bias, w1, w2):
    any_, vmem, smem = (pl.BlockSpec(memory_space=m) for m in (pl.ANY, pltpu.VMEM, pltpu.SMEM))
    dma = pltpu.SemaphoreType.DMA
    return pl.pallas_call(
        gather_kernel,
        out_shape=(
            jax.ShapeDtypeStruct((X, 2, 64, 4096), BF16),
            jax.ShapeDtypeStruct((X, 2, 64, 2560), BF16),
            jax.ShapeDtypeStruct((2, 320, 2560), BF16),
            jax.ShapeDtypeStruct((2, 320, 4096), BF16),
            jax.ShapeDtypeStruct((2, 8, 320), F32),
        ),
        in_specs=[smem, smem, smem, vmem, vmem, vmem, any_, any_, any_],
        out_specs=[any_] * 5,
        scratch_shapes=[
            pltpu.VMEM((2, 64, 4096), BF16),
            pltpu.VMEM((2, 64, 2560), BF16),
            pltpu.VMEM((CTX, 2, 64, 128), BF16),
            pltpu.VMEM((CTX, 2, 64, 128), BF16),
            dma((CTX,)), dma((CTX,)), dma((CTX,)), dma((CTX,)),
            dma((6,)), dma((5,)), dma((5,)), dma((4,)), dma((4,)), dma((4,)), dma((4,)),
        ],
        compiler_params=pltpu.CompilerParams(
            collective_id=0, has_side_effects=True, vmem_limit_bytes=40 * 2**20
        ),
        name="gather_rows",
    )(inv, order, frames, llm, vit, gain, bias, w1, w2)


def ring_sum(n, me, own, halves, bufs, accs, send, recv, to, finish):
    half = n // 2
    copies = []
    for d, sign in enumerate((1, -1)):
        t = lax.rem(me + n + sign * half, n)
        at = pl.ds(*halves[d])
        c = remote(own(t).at[at], bufs.at[d, 0, at], send.at[d, 0], recv.at[d, 0], to[d])
        c.start()
        copies.append(c)
    last = list(copies)
    yield
    for s in range(2, half + 1):
        for d, sign in enumerate((1, -1)):
            last[d].wait_recv()
            t = lax.rem(me + n + sign * (half + 1 - s), n)
            mine, came, out = own(t), bufs.at[d, s - 2], accs.at[d, s - 2]

            def add(i, mine=mine, came=came, out=out):
                out[i] = (mine[i].astype(F32) + came[i].astype(F32)).astype(BF16)

            def carry(i, mine=mine, out=out):
                out[i] = mine[i]

            if len(out.shape) == 2:
                if s == 2:
                    (a, an), (b, bn) = halves[d], halves[1 - d]
                    out[pl.ds(a, an)] = (
                        mine[pl.ds(a, an)].astype(F32) + came[pl.ds(a, an)].astype(F32)
                    ).astype(BF16)
                    out[pl.ds(b, bn)] = mine[pl.ds(b, bn)]
                else:
                    out[...] = (mine[...].astype(F32) + came[...].astype(F32)).astype(BF16)
            elif s == 2:
                (a, an), (b, bn) = halves[d], halves[1 - d]
                loop(an, lambda i, add=add, a=a: add(a + i))
                loop(bn, lambda i, carry=carry, b=b: carry(b + i))
            else:
                loop(out.shape[0], add)
            c = remote(out, bufs.at[d, s - 1], send.at[d, s - 1], recv.at[d, s - 1], to[d])
            c.start()
            copies.append(c)
            last[d] = c
        yield
    for d in range(2):
        last[d].wait_recv()
    finish(own(me), bufs.at[0, half - 1], bufs.at[1, half - 1])
    for c in copies:
        c.wait_send()


def scatter_kernel(
    ng, g1, g2, vit, gain,
    out_v, out1, out2,
    c1, c2, t1, t2, m1, m2, f1, f2, q1, q2,
    xb, xa, yb2, ya2, zb1, za1, zb2, za2, yb1, ya1,
    csend, crecv, xs, xr, ys2, yr2, zs1, zr1, zs2, zr2, ys1, yr1, qs, qr,
):
    x, y, z, core = place()
    x_to = [device(lax.rem(x + 1, X), y, z, core), device(lax.rem(x + X - 1, X), y, z, core)]
    y_to = [device(x, lax.rem(y + 1, Y), z, core), device(x, lax.rem(y + Y - 1, Y), z, core)]
    z_to = [device(x, y, lax.rem(z + 1, Z), core), device(x, y, lax.rem(z + Z - 1, Z), core)]
    sibling = device(x, y, z, 1 - core)
    z_lo = lax.rem(z, 2)
    swap = device(x, y, z + 1 - 2 * z_lo, 1 - core)
    barrier = greet(x_to + y_to + z_to + [sibling, swap])
    pl.semaphore_wait(barrier, 8)

    def finish_x(own, a, b):
        def rows(i):
            at = pl.ds(pl.multiple_of(i * 16, 16), 16)
            for block in range(2):
                for seg in range(4):
                    cols = slice(seg * SEG, (seg + 1) * SEG)
                    grad = (
                        own[block, at, cols].astype(F32)
                        + a[block, at, cols].astype(F32)
                        + b[block, at, cols].astype(F32)
                    )
                    states = vit[block, at, cols].astype(F32)
                    inv_rms = lax.rsqrt(jnp.mean(states * states, axis=-1, keepdims=True) + EPS)
                    scaled = states * inv_rms
                    g = grad * gain[...]
                    out_v[block, at, cols] = (
                        inv_rms * (g - scaled * jnp.mean(g * scaled, axis=-1, keepdims=True))
                    ).astype(BF16)

        loop(4, rows)

    xg = ring_sum(X, x, lambda t: ng.at[t], ((0, 1), (1, 1)), xb, xa, xs, xr, x_to, finish_x)
    next(xg)

    mine = lax.rem(z_lo + core, 2)
    pairs = []
    for k in range(4):
        yy = lax.rem(y + 2 + k, Y)
        pairs.append(remote(g2.at[1 - mine, yy], c2.at[yy], csend.at[k], crecv.at[k], sibling))
    pairs.append(remote(g1.at[1 - mine], c1, csend.at[4], crecv.at[4], sibling))
    for c in (pairs[0], pairs[4], pairs[1], pairs[2], pairs[3]):
        c.start()

    def fold2(k):
        yy = lax.rem(y + 2 + k, Y)
        pairs[k].wait_recv()

        def add(i):
            t2[yy, i] = (g2[mine, yy, i].astype(F32) + c2[yy, i].astype(F32)).astype(BF16)

        loop(Z, add)

    def fold1():
        pairs[4].wait_recv()

        def add(i):
            yy, zz = i // Z, lax.rem(i, Z)
            t1[zz, yy] = (g1[mine, yy, zz].astype(F32) + c1[yy, zz].astype(F32)).astype(BF16)

        loop(Y * Z, add)

    def keep2(own, a, b):
        def add(i):
            m2[i] = (own[i].astype(F32) + a[i].astype(F32) + b[i].astype(F32)).astype(BF16)

        loop(Z, add)

    def keep1(own, a, b):
        def add(i):
            m1[i] = (own[i].astype(F32) + a[i].astype(F32) + b[i].astype(F32)).astype(BF16)

        loop(Y, add)

    def last2(own, a, b):
        f2[...] = own[...].astype(F32) + a[...].astype(F32) + b[...].astype(F32)

    def last1(own, a, b):
        f1[...] = own[...].astype(F32) + a[...].astype(F32) + b[...].astype(F32)

    fold2(0)
    y2 = ring_sum(Y, y, lambda t: t2.at[t], ((0, 4), (4, 4)), yb2, ya2, ys2, yr2, y_to, keep2)
    next(y2)
    fold1()
    z1 = ring_sum(Z, z, lambda t: t1.at[t], ((0, 2), (2, 2)), zb1, za1, zs1, zr1, z_to, keep1)
    next(z1)
    for k in (1, 2, 3):
        fold2(k)
    next(z1)
    next(xg)
    next(z1)
    next(y2)
    next(z1)
    for _ in z1:
        pass
    y1 = ring_sum(Y, y, lambda t: m1.at[t], ((0, 48), (48, 32)), yb1, ya1, ys1, yr1, y_to, last1)
    next(y1)
    for _ in y2:
        pass
    z2 = ring_sum(Z, z, lambda t: m2.at[t], ((0, 64), (64, 64)), zb2, za2, zs2, zr2, z_to, last2)
    next(z2)
    next(y1)
    for _ in xg:
        pass
    next(z2)
    for _ in y1:
        pass
    for _ in z2:
        pass

    away = core != z_lo

    @pl.when(away)
    def _():
        q1[0] = f1[...].astype(BF16)
        q2[0] = f2[...].astype(BF16)
        a = remote(q1.at[0], q1.at[1], qs.at[0], qr.at[0], swap)
        b = remote(q2.at[0], q2.at[1], qs.at[1], qr.at[1], swap)
        a.start()
        b.start()
        a.wait()
        b.wait()
        out1[...] = q1[1].astype(F32)
        out2[...] = q2[1].astype(F32)

    @pl.when(jnp.logical_not(away))
    def _():
        out1[...] = f1[...]
        out2[...] = f2[...]

    for c in pairs:
        c.wait_send()


def scatter_sums(ng, g1, g2, vit, gain):
    vmem = pl.BlockSpec(memory_space=pltpu.VMEM)
    dma = pltpu.SemaphoreType.DMA
    v = pltpu.VMEM
    n = 320
    sems = []
    for steps in ((5,), (2, 2), (2, 2), (2, 4), (2, 4), (2, 2), (2,)):
        sems += [dma(steps), dma(steps)]
    return pl.pallas_call(
        scatter_kernel,
        out_shape=(
            jax.ShapeDtypeStruct((2, 64, 2560), BF16),
            jax.ShapeDtypeStruct((80, n), F32),
            jax.ShapeDtypeStruct((128, n), F32),
        ),
        in_specs=[vmem] * 5,
        out_specs=[vmem] * 3,
        scratch_shapes=[
            v((Y, Z, 80, n), BF16), v((Y, Z, 128, n), BF16),
            v((Z, Y, 80, n), BF16), v((Y, Z, 128, n), BF16),
            v((Y, 80, n), BF16), v((Z, 128, n), BF16),
            v((80, n), F32), v((128, n), F32),
            v((2, 80, n), BF16), v((2, 128, n), BF16),
            v((2, 2, 2, 64, 2560), BF16), v((2, 1, 2, 64, 2560), BF16),
            v((2, 2, Z, 128, n), BF16), v((2, 1, Z, 128, n), BF16),
            v((2, 4, Y, 80, n), BF16), v((2, 3, Y, 80, n), BF16),
            v((2, 4, 128, n), BF16), v((2, 3, 128, n), BF16),
            v((2, 2, 80, n), BF16), v((2, 1, 80, n), BF16),
        ] + sems,
        compiler_params=pltpu.CompilerParams(
            collective_id=1, has_side_effects=True, vmem_limit_bytes=56 * 2**20
        ),
        name="scatter_sums",
    )(ng, g1, g2, vit, gain)


def body(vit_states, norm_gain, w_first, b_first, w_second, llm_grad, block_order, frame_tokens):
    positions = jnp.arange(64, dtype=jnp.int32)
    matches = (block_order[None, :] == positions[:, None]).astype(jnp.int32)
    inverse = jnp.sum(matches * positions[None, :], axis=1)
    gain = norm_gain.reshape(1, SEG)
    llm_rows, n_rows, w1, w2, b = gather_rows(
        inverse, block_order, frame_tokens, llm_grad.reshape(2, 64, 4096), vit_states[0], gain,
        jnp.broadcast_to(b_first[None, :], (8, 320)), w_first, w_second,
    )
    grads = llm_rows.reshape(512, 4096)
    inputs = n_rows.reshape(512, 2560)
    contract_cols = (((1,), (1,)), ((), ()))
    contract_rows = (((0,), (0,)), ((), ()))
    dot = functools.partial(lax.dot_general, preferred_element_type=F32)
    first, second, ng = [], [], 0.0
    for h in range(2):
        pre_act = dot(inputs, w1[h], contract_cols) + b[h, :1]
        activated = gelu_value(pre_act).astype(BF16)
        hidden_grad = dot(grads, w2[h], contract_cols)
        pre_grad = (hidden_grad * gelu_slope(pre_act)).astype(BF16)
        second.append(dot(grads, activated, contract_rows).astype(BF16))
        first.append(dot(inputs, pre_grad, contract_rows).astype(BF16))
        ng = ng + dot(pre_grad, w1[h], (((1,), (0,)), ((), ())))
    g1 = jnp.stack(first).reshape(2, Y, Z, 80, 320)
    g2 = jnp.stack(second).reshape(2, Y, Z, 128, 320)
    vit_grad, first_grad, second_grad = scatter_sums(
        ng.astype(BF16).reshape(X, 2, 64, 2560), g1, g2, vit_states.reshape(2, 64, 2560), gain
    )
    return (vit_grad.reshape(1, ROWS, 2560), first_grad.T, second_grad.T)


def solution(mesh):
    placed = (
        P("dp", "ctx", None), P(), P("dp", None), P("dp"), P("dp", None), P("dp", "ctx", None), P(), P(),
    )
    return jax.shard_map(
        body,
        mesh=mesh,
        in_specs=placed,
        out_specs=(P("dp", "ctx", None), P("dp", "ctx"), P("dp", "ctx")),
        check_vma=False,
    )
```

time: 903 us -> 244 us (0.27)
  waiting for transfers between devices: 702 us -> 0 us
  Pallas kernels: 0 us -> 173 us
  local copies, waits for them, and re-layouts: 102 us -> 34 us
  starting transfers between devices: 33.4 us -> 0 us
  between operations: 14 us -> 0.77 us
  matrix products: 35.5 us -> 22.9 us
    all_gather x2 -> x0, waiting for transfers between devices: 300 us -> none  [the longest x1 199 us: body(): lax.all_gather(normed, 'dp', axis=0, tiled=True)]
    pallas_call x0 -> x2, Pallas kernels: none -> 173 us  [the longest x1 103 us: gather_rows(): pl.pallas_call(gather_kernel, out_shape=(jax.ShapeDtypeStruct((X, 2, 64,...]
    all_to_all x2 -> x0, waiting for transfers between devices: 172 us -> none  [the longest x1 149 us: body(): lax.all_to_all(stacked, 'ctx', split_axis=2, concat_axis=1, tiled=True)]
    reduce_scatter x2 -> x0, waiting for transfers between devices: 134 us -> none  [the longest x1 68.4 us: body(): lax.psum_scatter(first_local.astype(jnp.bfloat16), 'ctx', scatter_dimensi...]
    unnamed x6 -> x0, waiting for transfers between devices: 96.7 us -> none
    all_to_all x2 -> x0, starting transfers between devices: 33.2 us -> none  [the longest x1 23.6 us: body(): lax.all_to_all(ordered, 'ctx', split_axis=1, concat_axis=2, tiled=True)]
    select_n x1 -> x0, local copies, waits for them, and re-layouts: 25.1 us -> none  [body(): jnp.take(spread.reshape(groups, blocks, block_rows, -1), inverse, axis=1)]
    all_to_all x2 -> x0, local copies, waits for them, and re-layouts: 24.4 us -> none  [the longest x1 12.2 us: body(): lax.all_to_all(stacked, 'ctx', split_axis=2, concat_axis=1, tiled=True)]
  transfers between devices with their start and end apart: 7 -> 0, of which waited for: 7 -> 0; matrix products, arithmetic and copies ran while one was open for 4% -> 0% of each run, Pallas kernels for 0% -> 0%
where the time goes in v1:
time: 244 us; the launch traced here: 243 us
  Pallas kernels  173 us (71%)
  local copies, waits for them, and re-layouts  34 us (14%)
  matrix products  22.9 us (9%)
  other arithmetic  12.5 us (5%)
    pallas_call x1, Pallas kernels, gather_rows(): pl.pallas_call(gather_kernel, out_shape=(jax.ShapeDtypeStruct((X, 2, 64,...  103 us
    pallas_call x1, Pallas kernels, scatter_sums(): pl.pallas_call(scatter_kernel, out_shape=(jax.ShapeDtypeStruct((2, 64, 25...  70.2 us
    unnamed x39, local copies, waits for them, and re-layouts  15.7 us
    convert_element_type x2, local copies, waits for them, and re-layouts, body(): second.append(dot(grads, activated, contract_rows).astype(BF16))  9.23 us
    convert_element_type x2, local copies, waits for them, and re-layouts, body(): first.append(dot(inputs, pre_grad, contract_rows).astype(BF16))  7.64 us
    another operation x1, other arithmetic, body(): g2 = jnp.stack(second).reshape(2, Y, Z, 128, 320)  6.75 us
    dot_general x2, matrix products, body(): second.append(dot(grads, activated, contract_rows).astype(BF16))  6.15 us
    dot_general x2, matrix products, body(): hidden_grad = dot(grads, w2[h], contract_cols)  5.64 us

profile of v1, /device:TPU:1, one launch (start us, length us, event | category | flops | bytes accessed | tf_op | source)
XLA Modules:
  0.0 242.9 jit_solution(1118195300935139212)
XLA Ops:
  0.6 0.8 select_reduce_fusion.inv
  1.4 0.7 reshape.42.gain
  2.1 0.0 copy-start.4
  2.1 0.7 broadcast_in_dim.2.bias
  2.8 0.0 copy-start
  2.8 1.1 copy-done
  3.9 0.0 copy-start.1
  3.9 1.7 copy-done.1
  5.6 0.0 copy-start.2
  5.6 1.4 copy-done.2
  7.0 0.0 copy-start.3
  7.0 1.2 copy-done.3
  8.3 0.0 copy-start.5
  8.3 0.7 copy-done.5
  9.0 0.0 copy-start.6
  9.0 0.7 copy-done.6
  9.6 102.6 %gather_rows.1 = (bf16[4,2,64,4096]{3,2,1,0:T(8,128)(2,1)}, bf16[4,2,64,2560]{3,2,1,0:T(8,128)(2,1)S(1)}, bf16[2,320,2560]{2,1,0:T(8,128)(2,1)S(1)}, bf16[2,320,4096]{2,1,0:T(8,128)(2,1)}, f32[2,8,320]{2,1,0:T(8,128)S(1)}) custom-call(s32[64]{0:T(128)S(1)} %select_reduce_fusion.inv, s32[64]{0:T(128)S(1)} %copy-done.6, s32[8,128]{1,0:T(8,128)S(1)} %copy-done.5, ...), custom_call_target="tpu_custom_call" | custom-call | tf_op jit(solution)/shard_map/gather_rows/pallas_call | solution.py:235
  112.2 0.0 copy-start.11
  112.2 1.0 fusion.26
  113.3 0.0 copy-done.4
  113.3 0.0 copy-start.14
  113.3 0.8 copy-done.14
  114.1 0.8 copy-done.11
  114.9 4.0 %fusion.29 = bf16[512,320]{0,1:T(8,128)(2,1)S(1)} fusion(bf16[512,4096]{1,0:T(8,128)(2,1)} %bitcast.68, bf16[2,320,4096]{2,1,0:T(8,128)(2,1)S(1)} %copy-done.11, f32[512,320]{0,1:T(8,128)S(1)} %fusion.26), kind=kOutput, calls=%fused_computation.28 | convolution fusion | flops 1343815680 | bytes 7798784 | tf_op jit(solution)/shard_map/dot_general | solution.py:505
  118.9 0.0 copy-start.9
  118.9 0.0 copy-start.12
  118.9 1.0 fusion.23
  120.0 1.3 copy-done.12
  121.2 0.0 copy-start.16
  121.2 1.7 fusion.32
  122.9 0.0 copy-done.16
  122.9 0.0 copy-start.7
  122.9 0.7 copy-done.7
  123.6 2.2 convolution_convert_fusion.3
  125.8 0.0 copy-done.9
  125.8 2.2 convolution_convert_fusion.2
  128.0 3.8 %copy.17 = bf16[2560,320]{1,0:T(8,128)(2,1)} copy(bf16[2560,320]{0,1:T(8,128)(2,1)} %convolution_convert_fusion.2) | data formatting | bytes 3276800 | tf_op jit(solution)/shard_map/convert_element_type | solution.py:508
  131.8 3.8 %copy.16 = bf16[2560,320]{1,0:T(8,128)(2,1)} copy(bf16[2560,320]{0,1:T(8,128)(2,1)} %convolution_convert_fusion.3) | data formatting | bytes 3276800 | tf_op jit(solution)/shard_map/convert_element_type | solution.py:508
  135.6 0.0 copy-start.13
  135.6 0.0 copy-start.17
  135.6 5.0 %pad_maximum_fusion.1.g1 = bf16[2,4,8,80,320]{4,3,2,1,0:T(8,128)(2,1)} fusion(bf16[1,4,8,80,320]{4,3,2,1,0:T(8,128)(2,1)} %bitcast.63, bf16[1,4,8,80,320]{4,3,2,1,0:T(8,128)(2,1)} %bitcast.64), kind=kLoop, calls=%fused_computation.6 | loop fusion | flops 1638400 | bytes 6553600 | tf_op jit(solution)/shard_map/stack | solution.py:510
  140.7 0.0 copy-done.13
  140.7 0.0 copy-done.17
  140.7 0.0 copy-start.15
  140.7 3.1 %convolution_convert_fusion.1 = bf16[4096,320]{0,1:T(8,128)(2,1)} fusion(bf16[512,4096]{1,0:T(8,128)(2,1)S(1)} %bitcast.70, f32[512,320]{0,1:T(8,128)S(1)} %copy-done.17), kind=kOutput, calls=%fused_computation.2 | convolution fusion | flops 1344307200 | bytes 7471104 | tf_op jit(solution)/shard_map/dot_general | solution.py:507
  143.8 0.0 copy-done.15
  143.8 3.1 %convolution_convert_fusion = bf16[4096,320]{0,1:T(8,128)(2,1)} fusion(bf16[512,4096]{1,0:T(8,128)(2,1)S(1)} %bitcast.71, f32[512,320]{0,1:T(8,128)S(1)} %copy-done.15), kind=kOutput, calls=%fused_computation.1 | convolution fusion | flops 1344307200 | bytes 7471104 | tf_op jit(solution)/shard_map/dot_general | solution.py:507
  146.8 4.6 %copy.19 = bf16[4096,320]{1,0:T(8,128)(2,1)} copy(bf16[4096,320]{0,1:T(8,128)(2,1)} %convolution_convert_fusion) | data formatting | bytes 5242880 | tf_op jit(solution)/shard_map/convert_element_type | solution.py:507
  151.5 4.6 %copy.18 = bf16[4096,320]{1,0:T(8,128)(2,1)} copy(bf16[4096,320]{0,1:T(8,128)(2,1)} %convolution_convert_fusion.1) | data formatting | bytes 5242880 | tf_op jit(solution)/shard_map/convert_element_type | solution.py:507
  156.1 0.0 copy-start.8
  156.1 6.7 %pad_maximum_fusion.g2 = bf16[2,4,8,128,320]{4,3,2,1,0:T(8,128)(2,1)} fusion(bf16[1,4,8,128,320]{4,3,2,1,0:T(8,128)(2,1)} %bitcast.60, bf16[1,4,8,128,320]{4,3,2,1,0:T(8,128)(2,1)} %bitcast.61), kind=kLoop, calls=%fused_computation | loop fusion | flops 2621440 | bytes 10485760 | tf_op jit(solution)/shard_map/stack | solution.py:511
  162.8 0.0 copy-done.8
  162.8 0.0 copy-start.10
  162.8 1.5 fusion.9
  164.4 0.0 copy-done.10
  164.4 3.1 %add_convert_fusion = bf16[512,2560]{1,0:T(8,128)(2,1)} fusion(f32[512,2560]{1,0:T(8,128)S(1)} %fusion.9, bf16[512,320]{0,1:T(8,128)(2,1)S(1)} %copy-done.10, bf16[2,320,2560]{2,1,0:T(8,128)(2,1)S(1)} %get-tuple-element.14), kind=kOutput, calls=%fused_computation.3 | convolution fusion | flops 841482240 | bytes 9830400 | tf_op jit(solution)/shard_map/dot_general | solution.py:509
  167.5 70.2 %scatter_sums.1 = (bf16[2,64,2560]{2,1,0:T(8,128)(2,1)}, f32[80,320]{1,0:T(8,128)}, f32[128,320]{1,0:T(8,128)}) custom-call(bf16[4,2,64,2560]{3,2,1,0:T(8,128)(2,1)} %bitcast.62, bf16[2,4,8,80,320]{4,3,2,1,0:T(8,128)(2,1)} %pad_maximum_fusion.1.g1, bf16[2,4,8,128,320]{4,3,2,1,0:T(8,128)(2,1)} %pad_maximum_fusion.g2, bf16[2,64,2560]{2,1,0:T(8,128)(2,1)} %bitcast.53, ...), custom_call_target="tpu_custom_call" | custom-call | tf_op jit(solution)/shard_map/scatter_sums/pallas_call | solution.py:459
  237.7 1.7 copy.20
  239.4 2.0 copy.23
  241.4 1.6 copy.24
  (1 shorter events, 0.0 us)
Async XLA Ops:
  2.1 111.2 %copy-start.4 = (f32[1,640]{1,0:T(1,128)}, f32[1,640]{1,0:T(1,128)S(1)}, u32[]{:S(2)}) copy-start(f32[1,640]{1,0:T(1,128)S(1)} %reshape.42.gain) | copy-start | bytes 7684
  2.8 1.1 copy-start
  3.9 1.7 copy-start.1
  5.6 1.4 copy-start.2
  7.0 1.2 copy-start.3
  8.3 0.7 copy-start.5
  9.0 0.7 copy-start.6
  112.2 2.7 %copy-start.11 = (bf16[2,320,4096]{2,1,0:T(8,128)(2,1)S(1)}, bf16[2,320,4096]{2,1,0:T(8,128)(2,1)}, u32[]{:S(2)}) copy-start(bf16[2,320,4096]{2,1,0:T(8,128)(2,1)} %get-tuple-element.12) | copy-start | bytes 15728644
  113.3 0.8 copy-start.14
  118.9 6.9 %copy-start.9 = (bf16[512,320]{0,1:T(8,128)(2,1)}, bf16[512,320]{0,1:T(8,128)(2,1)S(1)}, u32[]{:S(2)}) copy-start(bf16[512,320]{0,1:T(8,128)(2,1)S(1)} %fusion.29) | copy-start | bytes 983044
  118.9 2.3 copy-start.12
  121.2 1.7 copy-start.16
  122.9 0.7 copy-start.7
  135.6 5.0 %copy-start.13 = (bf16[4,2,64,4096]{3,2,1,0:T(8,128)(2,1)S(1)}, bf16[4,2,64,4096]{3,2,1,0:T(8,128)(2,1)}, u32[]{:S(2)}) copy-start(bf16[4,2,64,4096]{3,2,1,0:T(8,128)(2,1)} %get-tuple-element.11) | copy-start | bytes 12582916
  135.6 5.0 %copy-start.17 = (f32[512,320]{0,1:T(8,128)S(1)}, f32[512,320]{0,1:T(8,128)}, u32[]{:S(2)}) copy-start(f32[512,320]{0,1:T(8,128)} %copy-done.16) | copy-start | bytes 1966084
  140.7 3.1 %copy-start.15 = (f32[512,320]{0,1:T(8,128)S(1)}, f32[512,320]{0,1:T(8,128)}, u32[]{:S(2)}) copy-start(f32[512,320]{0,1:T(8,128)} %copy-done.14) | copy-start | bytes 1966084
  156.1 6.8 %copy-start.8 = (bf16[512,320]{0,1:T(8,128)(2,1)S(1)}, bf16[512,320]{0,1:T(8,128)(2,1)}, u32[]{:S(2)}) copy-start(bf16[512,320]{0,1:T(8,128)(2,1)} %copy-done.7) | copy-start | bytes 983044
  162.8 1.6 copy-start.10

commit v2 on v0

v2 whole, which is shorter than its diff:
```python
import functools
import math

import jax
import jax.numpy as jnp
from jax import lax
from jax.experimental import pallas as pl
from jax.experimental.pallas import tpu as pltpu
from jax.sharding import PartitionSpec as P

MESH = pl.DeviceIdType.MESH
EPS = 1e-06
X, Y, Z, CTX = 4, 4, 8, 32
ROWS, SEG, HID, LLM, VIT = 128, 640, 320, 4096, 2560
HALF = LLM // 2
F32, BF16 = jnp.float32, jnp.bfloat16
NT = (((1,), (1,)), ((), ()))
NN = (((1,), (0,)), ((), ()))
TN = (((0,), (0,)), ((), ()))
dot = functools.partial(lax.dot_general, preferred_element_type=F32)


def place():
    dp, ctx = lax.axis_index("dp"), lax.axis_index("ctx")
    x, y, core = lax.rem(dp, X), ctx // 8, lax.rem(ctx, 2)
    z = lax.rem(ctx // 2, 4) * 2 + dp // X
    return x, y, z, core


def device(x, y, z, core):
    return (lax.rem(z, 2) * X + x, y * 8 + (z // 2) * 2 + core)


def remote(src, dst, send, recv, to):
    return pltpu.make_async_remote_copy(
        src_ref=src, dst_ref=dst, send_sem=send, recv_sem=recv, device_id=to, device_id_type=MESH
    )


def loop(n, body):
    lax.fori_loop(0, n, lambda i, c: (body(i), c)[1], 0)


def part(i, size):
    return pl.ds(pl.multiple_of(i * size, size), size)


def ring_sum(n, me, own, halves, step, bufs, accs, send, recv, to, finish):
    half = n // 2
    copies = []
    for d, sign in enumerate((1, -1)):
        t = lax.rem(me + n + sign * half, n)
        at = pl.ds(*halves[d])
        c = remote(own(t).at[at], bufs.at[d, 0, at], send.at[d, 0], recv.at[d, 0], to[d])
        c.start()
        copies.append(c)
    last = list(copies)
    yield
    for s in range(2, half + 1):
        for d, sign in enumerate((1, -1)):
            t = lax.rem(me + n + sign * (half + 1 - s), n)
            mine, came, out = own(t), bufs.at[d, s - 2], accs.at[d, s - 2]

            def add(first, count, came=came, mine=mine, out=out):
                def one(i):
                    at = pl.ds(pl.multiple_of(first + i * step, step), step)
                    out[at] = (mine[at].astype(F32) + came[at].astype(F32)).astype(BF16)

                loop(count // step, one)

            def carry(first, count, mine=mine, out=out):
                def one(i):
                    at = pl.ds(pl.multiple_of(first + i * step, step), step)
                    out[at] = mine[at]

                loop(count // step, one)

            if s == 2:
                carry(*halves[1 - d])
                last[d].wait_recv()
                add(*halves[d])
            else:
                last[d].wait_recv()
                add(0, out.shape[0])
            c = remote(out, bufs.at[d, s - 1], send.at[d, s - 1], recv.at[d, s - 1], to[d])
            c.start()
            copies.append(c)
            last[d] = c
        yield
    for d in range(2):
        last[d].wait_recv()
    finish(own(me), bufs.at[0, half - 1], bufs.at[1, half - 1])
    for c in copies:
        c.wait_send()


def kernel(
    inv, order, frames, llm, vit, gain, bias, w1, w2,
    out_v, out1, out2,
    masked, recv1a, recv1b, send2, n_rows, l_rows, w1v, w2v, bv,
    pre, hg, act, pg, ng,
    g1, c1, t1, g2, c2, t2,
    m1, m2, f1, f2, q1, q2,
    xb, xa, y1b, y1a, z1b, z1a, z2b, z2a, y2b, y2a,
    s1, r1, s2, r2, loc, wsend, wrecv, nsend, nrecv, lsend, lrecv, esend, erecv,
    xs, xr, y1s, y1r, z1s, z1r, z2s, z2r, y2s, y2r, qs, qr,
):
    recv1 = (recv1a, recv1b)
    x, y, z, core = place()
    ctx, dp = lax.axis_index("ctx"), lax.axis_index("dp")
    right, left, far = lax.rem(x + 1, X), lax.rem(x + X - 1, X), lax.rem(x + 2, X)
    up, down = lax.rem(z + 1, Z), lax.rem(z + Z - 1, Z)
    x_to = [device(right, y, z, core), device(left, y, z, core)]
    y_to = [device(x, lax.rem(y + 1, Y), z, core), device(x, lax.rem(y + Y - 1, Y), z, core)]
    z_to = [device(x, y, up, core), device(x, y, down, core)]
    sibling = device(x, y, z, 1 - core)
    z_lo, z_hi = lax.rem(z, 2), z // 2
    swap = device(x, y, z + 1 - 2 * z_lo, 1 - core)

    barrier = pltpu.get_barrier_semaphore()

    def hello(k):
        pl.semaphore_signal(
            barrier, inc=1, device_id=(dp, lax.rem(ctx + k + 1, CTX)), device_id_type=MESH
        )

    loop(CTX - 1, hello)
    for other in x_to + z_to + [swap]:
        pl.semaphore_signal(barrier, inc=1, device_id=other, device_id_type=MESH)

    keep_w = [
        pltpu.make_async_copy(w1, w1v.at[pl.ds(0, HID)], loc.at[0]),
        pltpu.make_async_copy(w2, w2v.at[pl.ds(0, HID)], loc.at[1]),
        pltpu.make_async_copy(bias, bv.at[pl.ds(0, HID)], loc.at[2]),
    ]
    for c in keep_w:
        c.start()

    def norm(i):
        rows = part(i, 32)
        for seg in range(4):
            cols = slice(seg * SEG, (seg + 1) * SEG)
            states = vit[rows, cols].astype(F32)
            inv_rms = lax.rsqrt(jnp.mean(states * states, axis=-1, keepdims=True) + EPS)
            n_rows[x, rows, cols] = (states * inv_rms * gain[...]).astype(BF16)

    loop(4, norm)

    t0 = order[2 * ctx]
    t1_ = order[2 * ctx + 1]
    low_first = lax.rem(t0 // 4, 4) < 2
    for b in range(2):
        at_first = low_first if b == 0 else jnp.logical_not(low_first)
        index = jnp.where(at_first, 0, 1)
        t = jnp.where(at_first, t0, t1_)
        for frame in range(2):
            count = frames[dp, 2 * t + frame]
            keep = lax.broadcasted_iota(jnp.int32, (32, 512), 0) < count
            rows = pl.ds(32 * frame, 32)

            def mask(c, b=b, index=index, keep=keep, rows=rows):
                cols = part(c, 512)
                masked[b, rows, cols] = jnp.where(
                    keep, llm[index, rows, cols].astype(F32), 0.0
                ).astype(BF16)

            loop(8, mask)

    pl.semaphore_wait(barrier, CTX - 1 + 5)

    def spread(rows, cols, send, recv):
        own = rows.at[x, :, cols]
        return [remote(own, own, send.at[d], recv.at[d], x_to[d]) for d in range(2)]

    def forward(rows, cols, send, recv):
        out = []
        for d, slot in enumerate((left, right)):
            piece = rows.at[slot, pl.ds(64 * d, 64), cols]
            out.append(remote(piece, piece, send.at[2 + d], recv.at[2 + d], x_to[d]))
        return out

    def start(copies):
        for c in copies:
            c.start()

    def received(copies):
        for c in copies:
            c.wait_recv()

    all_n = pl.ds(0, VIT)
    n_a = spread(n_rows, all_n, nsend, nrecv)
    start(n_a)

    def q_of(m):
        return (m // 8) * 4 + lax.rem(m, 4)

    def b_of(m):
        return lax.rem(m // 4, 2)

    q = q_of(ctx)

    def strip(h, k):
        return pl.ds(pl.multiple_of(h * HALF + k * 128, 128), 128)

    def first(h, k):
        m = lax.rem(ctx + k + 1, CTX)
        return remote(
            masked.at[b_of(m), :, strip(h, q_of(m))], recv1[h].at[ctx], s1.at[h, k], r1.at[h, ctx], (dp, m)
        )

    def first_here(h, k):
        s = lax.rem(ctx + k + 1, CTX)
        return remote(masked.at[0, :, strip(h, 0)], recv1[h].at[s], s1.at[h, k], r1.at[h, s], (dp, s))

    own1 = [
        pltpu.make_async_copy(masked.at[b_of(ctx), :, strip(h, q)], recv1[h].at[ctx], loc.at[3 + h])
        for h in range(2)
    ]
    for h in range(2):
        loop(CTX - 1, lambda k, h=h: first(h, k).start())
        own1[h].start()

    def owner(e):
        return (e // 4) * 8 + b_of(ctx) * 4 + lax.rem(e, 4)

    def pick(h, e):
        for i in range(2):
            block = inv[2 * owner(e) + i]
            send2[h, e, pl.ds(64 * i, 64)] = recv1[h][block // 2]

    def second(h, k):
        e = lax.rem(q + k + 1, 16)
        return remote(
            send2.at[h, e], l_rows.at[x, :, strip(h, q)], s2.at[h, k], r2.at[h, q], (dp, owner(e))
        )

    def second_here(h, k):
        e = lax.rem(q + k + 1, 16)
        return remote(
            send2.at[h, e], l_rows.at[x, :, strip(h, e)], s2.at[h, k], r2.at[h, e], (dp, owner(e))
        )

    own2 = [
        pltpu.make_async_copy(send2.at[h, q], l_rows.at[x, :, strip(h, q)], loc.at[5 + h])
        for h in range(2)
    ]

    def reorder(h):
        loop(CTX - 1, lambda k: first_here(h, k).wait_recv())
        own1[h].wait()

        def send(k):
            pick(h, lax.rem(q + k + 1, 16))
            second(h, k).start()

        loop(15, send)
        pick(h, q)
        own2[h].start()

    def reordered(h):
        loop(15, lambda k: second_here(h, k).wait_recv())
        own2[h].wait()

    to_z = device(x, y, jnp.where(core == 0, up, down), core)
    mine_w = pl.ds(pl.multiple_of(core * 160, 32), 160)
    there_w = pl.ds(pl.multiple_of(HID + core * 160, 32), 160)
    other_w = pl.ds(HID, HID)
    w_a = [
        remote(w1.at[mine_w], w1v.at[there_w], wsend.at[0], wrecv.at[0], to_z),
        remote(bias, bv.at[other_w], wsend.at[1], wrecv.at[1], to_z),
    ]
    w_b = [remote(w2.at[mine_w], w2v.at[there_w], wsend.at[2], wrecv.at[2], to_z)]
    w_c = [remote(w1v.at[there_w], w1v.at[there_w], wsend.at[3], wrecv.at[3], sibling)]
    w_d = [remote(w2v.at[there_w], w2v.at[there_w], wsend.at[4], wrecv.at[4], sibling)]

    def group(k):
        return pl.ds(k * HID, HID)

    def activate(k):
        pre[group(k)] = dot(w1v[group(k)], n_rows[...].reshape(X * ROWS, VIT), NT)

        def chunk(i):
            at = pl.ds(pl.multiple_of(k * HID + i * 32, 32), 32)
            v = pre[at] + bv[at, :1]
            cdf = 0.5 * (1.0 + lax.erf(v * (1.0 / math.sqrt(2.0))))
            density = jnp.exp(-0.5 * v * v) * (1.0 / math.sqrt(2.0 * math.pi))
            act[at] = (v * cdf).astype(BF16)
            pre[at] = cdf + v * density

        loop(10, chunk)

    def tokens(slot):
        return part(slot, ROWS)

    def hidden(slot, h, k):
        cols = pl.ds(h * HALF, HALF)
        got = dot(w2v[group(k), cols], l_rows[slot, :, cols], NT)
        if h == 0:
            hg[group(k), tokens(slot)] = got
        else:
            hg[group(k), tokens(slot)] += got

    def gradient(slot):
        def chunk(i):
            at = part(i, 64)
            pg[at, tokens(slot)] = (hg[at, tokens(slot)] * pre[at, tokens(slot)]).astype(BF16)

        loop(10, chunk)
        for c in range(2):
            cols = slice(c * 1280, (c + 1) * 1280)
            ng[slot, :, cols] = dot(pg[:, tokens(slot)], w1v[:, cols], TN).astype(BF16)

    mine = lax.rem(z_lo + core, 2)
    own_h, other_h = (pl.ds(pl.multiple_of(k * HID, HID), HID) for k in (mine, 1 - mine))

    def second_grad(h, at, into):
        for c in range(4):
            cols = slice(h * HALF + c * 512, h * HALF + (c + 1) * 512)
            got = dot(act[at], l_rows[:, :, cols].reshape(X * ROWS, 512), NN).astype(BF16)
            for i in range(4):
                into[h, (4 * c + i) % Z, c // 2] = got[:, i * 128 : (i + 1) * 128]

    def first_grad(at, into):
        for yy in range(Y):
            got = dot(pg[at], n_rows[:, :, yy * SEG : (yy + 1) * SEG].reshape(X * ROWS, SEG), NN)
            into[yy] = got.astype(BF16)

    e2 = [remote(g2.at[h], c2.at[h], esend.at[h], erecv.at[h], sibling) for h in range(2)]
    e1 = remote(g1, c1, esend.at[2], erecv.at[2], sibling)

    def fold2(h):
        e2[h].wait_recv()

        def add(i):
            at = (h, i // 2, lax.rem(i, 2))
            t2[at] = (t2[at].astype(F32) + c2[at].astype(F32)).astype(BF16)

        loop(2 * Z, add)

    def fold1():
        e1.wait_recv()

        def add(i):
            at = (i // 5, part(lax.rem(i, 5), 64))
            t1[at] = (t1[at].astype(F32) + c1[at].astype(F32)).astype(BF16)

        loop(5 * Y, add)

    def keep2(h):
        def finish(own, a, b):
            for i in range(2):
                m2[2 * h + i] = (
                    own[i].astype(F32) + a[i].astype(F32) + b[i].astype(F32)
                ).astype(BF16)

        return finish

    def keep1(own, a, b):
        for c in range(5):
            cols = slice(c * 128, (c + 1) * 128)
            total = own[:, cols].astype(F32) + a[:, cols].astype(F32) + b[:, cols].astype(F32)
            m1[cols] = total.T.astype(BF16)

    def last(f):
        def finish(own, a, b):
            f[...] = own[...].astype(F32) + a[...].astype(F32) + b[...].astype(F32)

        return finish

    def finish_x(own, a, b):
        def rows(i):
            at = part(i, 16)
            for seg in range(4):
                cols = slice(seg * SEG, (seg + 1) * SEG)
                grad = (
                    own[at, cols].astype(F32) + a[at, cols].astype(F32) + b[at, cols].astype(F32)
                )
                states = vit[at, cols].astype(F32)
                inv_rms = lax.rsqrt(jnp.mean(states * states, axis=-1, keepdims=True) + EPS)
                scaled = states * inv_rms
                g = grad * gain[...]
                out_v[at, cols] = (
                    inv_rms * (g - scaled * jnp.mean(g * scaled, axis=-1, keepdims=True))
                ).astype(BF16)

        loop(8, rows)

    x_ring = ring_sum(
        X, x, lambda t: ng.at[t], ((0, 64), (64, 64)), 16, xb, xa, xs, xr, x_to, finish_x
    )
    z2_rings = [
        ring_sum(
            Z, z, lambda t, h=h: t2.at[h, t], ((0, 1), (1, 1)), 1,
            z2b.at[h], z2a.at[h], z2s.at[h], z2r.at[h], z_to, keep2(h),
        )
        for h in range(2)
    ]
    y2_ring = ring_sum(
        Y, y, lambda t: m2.at[t], ((0, 160), (160, 160)), 160, y2b, y2a, y2s, y2r, y_to, last(f2)
    )
    y1_ring = ring_sum(
        Y, y, lambda t: t1.at[t], ((0, 160), (160, 160)), 32, y1b, y1a, y1s, y1r, y_to, keep1
    )
    z1_ring = ring_sum(
        Z, z, lambda t: m1.at[part(t, 80)], ((0, 48), (48, 32)), 16, z1b, z1a, z1s, z1r, z_to, last(f1)
    )

    def run(*rings):
        for r in rings:
            next(r, None)

    l_cols = [pl.ds(h * HALF, HALF) for h in range(2)]
    l_a = [spread(l_rows, l_cols[h], lsend.at[h], lrecv.at[h]) for h in range(2)]
    l_f = [forward(l_rows, l_cols[h], lsend.at[h], lrecv.at[h]) for h in range(2)]
    n_f = forward(n_rows, all_n, nsend, nrecv)

    reorder(0)
    received(n_a)
    start(n_f)
    start(w_a)
    reorder(1)
    start(w_b)
    reordered(0)
    start(l_a[0])
    received(n_f)
    for c in keep_w:
        c.wait()
    activate(0)
    reordered(1)
    start(l_a[1])
    hidden(x, 0, 0)
    received(l_a[0])
    start(l_f[0])
    received(w_a)
    start(w_c)
    for slot in (left, right):
        hidden(slot, 0, 0)
    hidden(x, 1, 0)
    received(w_c)
    activate(1)
    received(l_a[1])
    start(l_f[1])
    received(l_f[0])
    second_grad(0, other_h, g2)
    e2[0].start()
    second_grad(0, own_h, t2)
    received(w_b)
    start(w_d)
    hidden(far, 0, 0)
    for slot in (left, right):
        hidden(slot, 1, 0)
    fold2(0)
    run(z2_rings[0])
    received(w_d)
    for slot in (x, left, right, far):
        hidden(slot, 0, 1)
    for slot in (x, left, right):
        hidden(slot, 1, 1)
    received(l_f[1])
    hidden(far, 1, 0)
    hidden(far, 1, 1)
    gradient(far)
    run(x_ring)
    run(z2_rings[0])
    gradient(left)
    gradient(right)
    gradient(x)
    first_grad(other_h, g1)
    e1.start()
    second_grad(1, other_h, g2)
    e2[1].start()
    run(x_ring)
    first_grad(own_h, t1)
    run(z2_rings[0])
    second_grad(1, own_h, t2)
    fold1()
    run(y1_ring)
    fold2(1)
    run(z2_rings[1])
    run(z2_rings[0])
    run(z2_rings[1])
    run(y1_ring)
    run(z2_rings[0])
    run(z2_rings[1])
    run(y1_ring)
    run(z1_ring)
    run(z2_rings[1])
    run(z1_ring)
    run(x_ring)
    run(z1_ring)
    run(z2_rings[1])
    run(y2_ring)
    run(z1_ring)
    run(y2_ring)
    run(z1_ring)
    run(y2_ring)

    away = core != z_lo

    @pl.when(away)
    def _():
        q1[0] = f1[...].astype(BF16)
        q2[0] = f2[...].astype(BF16)
        a = remote(q1.at[0], q1.at[1], qs.at[0], qr.at[0], swap)
        b = remote(q2.at[0], q2.at[1], qs.at[1], qr.at[1], swap)
        a.start()
        b.start()
        a.wait()
        b.wait()
        out1[...] = q1[1].astype(F32)
        out2[...] = q2[1].astype(F32)

    @pl.when(jnp.logical_not(away))
    def _():
        out1[...] = f1[...]
        out2[...] = f2[...]

    for c in n_a + n_f + l_a[0] + l_a[1] + l_f[0] + l_f[1] + w_a + w_b + w_c + w_d + e2 + [e1]:
        c.wait_send()
    for h in range(2):
        loop(CTX - 1, lambda k, h=h: first(h, k).wait_send())
        loop(15, lambda k, h=h: second(h, k).wait_send())


def fused(inv, order, frames, llm, vit, gain, bias, w1, w2):
    any_, vmem, smem = (pl.BlockSpec(memory_space=m) for m in (pl.ANY, pltpu.VMEM, pltpu.SMEM))
    dma = pltpu.SemaphoreType.DMA

    def v(*shape, dtype=BF16):
        return pltpu.VMEM(shape, dtype)

    f32 = functools.partial(v, dtype=F32)
    pairs = [(2, CTX), (2, 16)]
    sems = []
    for shape in pairs:
        sems += [dma(shape), dma(shape)]
    sems += [dma((7,))]
    for shape in ((5,), (4,), (2, 4), (3,), (2, 2), (2, 2), (2, 4), (2, 2, 4), (2, 2), (2,)):
        sems += [dma(shape), dma(shape)]
    return pl.pallas_call(
        kernel,
        out_shape=(
            jax.ShapeDtypeStruct((ROWS, VIT), BF16),
            jax.ShapeDtypeStruct((80, HID), F32),
            jax.ShapeDtypeStruct((HID, 128), F32),
        ),
        in_specs=[smem, smem, smem, vmem, vmem, vmem, any_, any_, any_],
        out_specs=[vmem] * 3,
        scratch_shapes=[
            v(2, 64, LLM), v(CTX, 64, 128), v(CTX, 64, 128), v(2, 16, ROWS, 128),
            v(X, ROWS, VIT), v(X, ROWS, LLM),
            v(2 * HID, VIT), v(2 * HID, LLM), f32(2 * HID, 128),
            f32(2 * HID, X * ROWS), f32(2 * HID, X * ROWS),
            v(2 * HID, X * ROWS), v(2 * HID, X * ROWS), v(X, ROWS, VIT),
            v(Y, HID, SEG), v(Y, HID, SEG), v(Y, HID, SEG),
            v(2, Z, 2, HID, 128), v(2, Z, 2, HID, 128), v(2, Z, 2, HID, 128),
            v(SEG, HID), v(Y, HID, 128), f32(80, HID), f32(HID, 128),
            v(2, 80, HID), v(2, HID, 128),
            v(2, 2, ROWS, VIT), v(2, 1, ROWS, VIT),
            v(2, 2, HID, SEG), v(2, 1, HID, SEG),
            v(2, 4, 80, HID), v(2, 3, 80, HID),
            v(2, 2, 4, 2, HID, 128), v(2, 2, 3, 2, HID, 128),
            v(2, 2, HID, 128), v(2, 1, HID, 128),
        ] + sems,
        compiler_params=pltpu.CompilerParams(
            collective_id=0, has_side_effects=True, vmem_limit_bytes=60 * 2**20
        ),
        name="fused",
    )(inv, order, frames, llm, vit, gain, bias, w1, w2)


def body(vit_states, norm_gain, w_first, b_first, w_second, llm_grad, block_order, frame_tokens):
    positions = jnp.arange(64, dtype=jnp.int32)
    matches = (block_order[None, :] == positions[:, None]).astype(jnp.int32)
    inverse = jnp.sum(matches * positions[None, :], axis=1)
    vit_grad, first, second = fused(
        inverse, block_order, frame_tokens, llm_grad.reshape(2, 64, LLM), vit_states[0],
        norm_gain.reshape(1, SEG), jnp.broadcast_to(b_first[:, None], (HID, 128)), w_first, w_second,
    )
    return (vit_grad[None], first.T, second)


def solution(mesh):
    placed = (
        P("dp", "ctx", None), P(), P("dp", None), P("dp"), P("dp", None), P("dp", "ctx", None), P(), P(),
    )
    return jax.shard_map(
        body,
        mesh=mesh,
        in_specs=placed,
        out_specs=(P("dp", "ctx", None), P("dp", "ctx"), P("dp", "ctx")),
        check_vma=False,
    )
```

time: 903 us -> 165 us (0.18)
  waiting for transfers between devices: 702 us -> 0 us
  Pallas kernels: 0 us -> 154 us
  local copies, waits for them, and re-layouts: 102 us -> 7.84 us
  matrix products: 35.5 us -> 0 us
  starting transfers between devices: 33.4 us -> 0 us
  other arithmetic: 14.9 us -> 1.28 us
  between operations: 14 us -> 0.64 us
    all_gather x2 -> x0, waiting for transfers between devices: 300 us -> none  [the longest x1 199 us: body(): lax.all_gather(normed, 'dp', axis=0, tiled=True)]
    all_to_all x2 -> x0, waiting for transfers between devices: 172 us -> none  [the longest x1 149 us: body(): lax.all_to_all(stacked, 'ctx', split_axis=2, concat_axis=1, tiled=True)]
    pallas_call x0 -> x1, Pallas kernels: none -> 154 us  [fused(): pl.pallas_call(kernel, out_shape=(jax.ShapeDtypeStruct((ROWS, VIT), BF16)...]
    reduce_scatter x2 -> x0, waiting for transfers between devices: 134 us -> none  [the longest x1 68.4 us: body(): lax.psum_scatter(first_local.astype(jnp.bfloat16), 'ctx', scatter_dimensi...]
    unnamed x6 -> x0, waiting for transfers between devices: 96.7 us -> none
    dot_general x5 -> x0, matrix products: 35.5 us -> none  [the longest x1 9.38 us: body(): lax.dot_general(masked, w_second, contract_cols, preferred_element_type=j...]
    all_to_all x2 -> x0, starting transfers between devices: 33.2 us -> none  [the longest x1 23.6 us: body(): lax.all_to_all(ordered, 'ctx', split_axis=1, concat_axis=2, tiled=True)]
    select_n x1 -> x0, local copies, waits for them, and re-layouts: 25.1 us -> none  [body(): jnp.take(spread.reshape(groups, blocks, block_rows, -1), inverse, axis=1)]
  transfers between devices with their start and end apart: 7 -> 0, of which waited for: 7 -> 0; matrix products, arithmetic and copies ran while one was open for 4% -> 0% of each run, Pallas kernels for 0% -> 0%
where the time goes in v2:
time: 165 us; the launch traced here: 164 us
  Pallas kernels  154 us (93%)
  local copies, waits for them, and re-layouts  7.84 us (5%)
    pallas_call x1, Pallas kernels, fused(): pl.pallas_call(kernel, out_shape=(jax.ShapeDtypeStruct((ROWS, VIT), BF16)...  154 us
    unnamed x3, local copies, waits for them, and re-layouts  5.11 us

profile of v2, /device:TPU:1, one launch (start us, length us, event | category | flops | bytes accessed | tf_op | source)
XLA Modules:
  0.0 164.2 jit_solution(5181830049108498257)
XLA Ops:
  0.6 1.3 select_reduce_fusion.inv
  1.9 1.3 reshape.15.gain
  3.2 1.5 broadcast_in_dim.4.bias
  4.6 154.5 %fused.1 = (bf16[128,2560]{1,0:T(8,128)(2,1)}, f32[80,320]{1,0:T(8,128)}, f32[320,128]{1,0:T(8,128)}) custom-call(s32[64]{0:T(128)} %select_reduce_fusion.inv, s32[64]{0:T(128)} %order.1, s32[8,128]{1,0:T(8,128)} %frames.1, bf16[2,64,4096]{2,1,0:T(8,128)(2,1)} %bitcast.4, bf16[128,2560]{1,0:T(8,128)(2,1)} %bitcast.6, f32[1,640]{1,0:T(1,128)} %reshape.15.gain, ...), custom_call_target="tpu_custom_call" | custom-call | tf_op jit(solution)/shard_map/fused/pallas_call | solution.py:540
  159.1 2.0 %copy.14 = bf16[1,128,2560]{2,1,0:T(8,128)(2,1)} copy(bf16[1,128,2560]{2,1,0:T(8,128)(2,1)} %bitcast.5) | data formatting | bytes 1310720
  161.1 1.6 copy.15
  162.7 1.6 copy.16

commit v3 on v2

--- a/solution.py
+++ b/solution.py
@@ -13,6 +13,7 @@
 X, Y, Z, CTX = 4, 4, 8, 32
 ROWS, SEG, HID, LLM, VIT = 128, 640, 320, 4096, 2560
 HALF = LLM // 2
+CHUNKS = tuple((h, pl.ds(r, 32)) for h in range(2) for r in (0, 32))
 F32, BF16 = jnp.float32, jnp.bfloat16
 NT = (((1,), (1,)), ((), ()))
 NN = (((1,), (0,)), ((), ()))
@@ -97,15 +98,15 @@
 def kernel(
     inv, order, frames, llm, vit, gain, bias, w1, w2,
     out_v, out1, out2,
-    masked, recv1a, recv1b, send2, n_rows, l_rows, w1v, w2v, bv,
+    masked, recv1a, recv1b, recv1c, recv1d, send2a, send2b, send2c, send2d, n_rows, l_rows, w1v, w2v, bv,
     pre, hg, act, pg, ng,
-    g1, c1, t1, g2, c2, t2,
+    act_s, pg_s, t1, t2,
     m1, m2, f1, f2, q1, q2,
     xb, xa, y1b, y1a, z1b, z1a, z2b, z2a, y2b, y2a,
-    s1, r1, s2, r2, loc, wsend, wrecv, nsend, nrecv, lsend, lrecv, esend, erecv,
+    s1, r1, s2, r2, loc, wsend, wrecv, nsend, nrecv, lsend, lrecv, csend, crecv,
     xs, xr, y1s, y1r, z1s, z1r, z2s, z2r, y2s, y2r, qs, qr,
 ):
-    recv1 = (recv1a, recv1b)
+    recv1, send2 = (recv1a, recv1b, recv1c, recv1d), (send2a, send2b, send2c, send2d)
     x, y, z, core = place()
     ctx, dp = lax.axis_index("ctx"), lax.axis_index("dp")
     right, left, far = lax.rem(x + 1, X), lax.rem(x + X - 1, X), lax.rem(x + 2, X)
@@ -131,10 +132,11 @@
     keep_w = [
         pltpu.make_async_copy(w1, w1v.at[pl.ds(0, HID)], loc.at[0]),
         pltpu.make_async_copy(w2, w2v.at[pl.ds(0, HID)], loc.at[1]),
-        pltpu.make_async_copy(bias, bv.at[pl.ds(0, HID)], loc.at[2]),
     ]
     for c in keep_w:
         c.start()
+
+    bv[pl.ds(0, HID)] = jnp.broadcast_to(bias[...][None, :], (128, HID)).T
 
     def norm(i):
         rows = part(i, 32)
@@ -142,7 +144,9 @@
             cols = slice(seg * SEG, (seg + 1) * SEG)
             states = vit[rows, cols].astype(F32)
             inv_rms = lax.rsqrt(jnp.mean(states * states, axis=-1, keepdims=True) + EPS)
-            n_rows[x, rows, cols] = (states * inv_rms * gain[...]).astype(BF16)
+            n_rows[0, x, i // 2, part(lax.rem(i, 2), 32), cols] = (
+                states * inv_rms * gain[...][None, :]
+            ).astype(BF16)
 
     loop(4, norm)
 
@@ -168,15 +172,15 @@
 
     pl.semaphore_wait(barrier, CTX - 1 + 5)
 
-    def spread(rows, cols, send, recv):
-        own = rows.at[x, :, cols]
+    def spread(piece, send, recv):
+        own = piece(x, slice(0, 2))
         return [remote(own, own, send.at[d], recv.at[d], x_to[d]) for d in range(2)]
 
-    def forward(rows, cols, send, recv):
+    def forward(piece, send, recv):
         out = []
         for d, slot in enumerate((left, right)):
-            piece = rows.at[slot, pl.ds(64 * d, 64), cols]
-            out.append(remote(piece, piece, send.at[2 + d], recv.at[2 + d], x_to[d]))
+            one = piece(slot, d)
+            out.append(remote(one, one, send.at[2 + d], recv.at[2 + d], x_to[d]))
         return out
 
     def start(copies):
@@ -187,9 +191,11 @@
         for c in copies:
             c.wait_recv()
 
-    all_n = pl.ds(0, VIT)
-    n_a = spread(n_rows, all_n, nsend, nrecv)
-    start(n_a)
+    def n_piece(slot, block):
+        return n_rows.at[0, slot, block]
+
+    n_a = spread(n_piece, nsend, nrecv)
+    n_f = forward(n_piece, nsend, nrecv)
 
     def q_of(m):
         return (m // 8) * 4 + lax.rem(m, 4)
@@ -202,82 +208,106 @@
     def strip(h, k):
         return pl.ds(pl.multiple_of(h * HALF + k * 128, 128), 128)
 
-    def first(h, k):
+    def first(c, k):
+        h, rows = CHUNKS[c]
         m = lax.rem(ctx + k + 1, CTX)
         return remote(
-            masked.at[b_of(m), :, strip(h, q_of(m))], recv1[h].at[ctx], s1.at[h, k], r1.at[h, ctx], (dp, m)
+            masked.at[b_of(m), rows, strip(h, q_of(m))], recv1[c].at[ctx], s1.at[c, k], r1.at[c, ctx], (dp, m)
         )
 
-    def first_here(h, k):
+    def first_here(c, k):
+        h, rows = CHUNKS[c]
         s = lax.rem(ctx + k + 1, CTX)
-        return remote(masked.at[0, :, strip(h, 0)], recv1[h].at[s], s1.at[h, k], r1.at[h, s], (dp, s))
+        return remote(masked.at[0, rows, strip(h, 0)], recv1[c].at[s], s1.at[c, k], r1.at[c, s], (dp, s))
 
     own1 = [
-        pltpu.make_async_copy(masked.at[b_of(ctx), :, strip(h, q)], recv1[h].at[ctx], loc.at[3 + h])
-        for h in range(2)
+        pltpu.make_async_copy(masked.at[b_of(ctx), rows, strip(h, q)], recv1[c].at[ctx], loc.at[2 + c])
+        for c, (h, rows) in enumerate(CHUNKS)
     ]
-    for h in range(2):
-        loop(CTX - 1, lambda k, h=h: first(h, k).start())
-        own1[h].start()
+
+    def offer(c):
+        loop(CTX - 1, lambda k: first(c, k).start())
+        own1[c].start()
 
     def owner(e):
         return (e // 4) * 8 + b_of(ctx) * 4 + lax.rem(e, 4)
 
-    def pick(h, e):
+    def pick(c, e):
         for i in range(2):
             block = inv[2 * owner(e) + i]
-            send2[h, e, pl.ds(64 * i, 64)] = recv1[h][block // 2]
-
-    def second(h, k):
+            send2[c][e, i] = recv1[c][block // 2]
+
+    def landing(c, k):
+        h, rows = CHUNKS[c]
+        return l_rows.at[0, x, :, rows, strip(h, k)]
+
+    def second(c, k):
         e = lax.rem(q + k + 1, 16)
-        return remote(
-            send2.at[h, e], l_rows.at[x, :, strip(h, q)], s2.at[h, k], r2.at[h, q], (dp, owner(e))
-        )
-
-    def second_here(h, k):
+        return remote(send2[c].at[e], landing(c, q), s2.at[c, k], r2.at[c, q], (dp, owner(e)))
+
+    def second_here(c, k):
         e = lax.rem(q + k + 1, 16)
-        return remote(
-            send2.at[h, e], l_rows.at[x, :, strip(h, e)], s2.at[h, k], r2.at[h, e], (dp, owner(e))
-        )
+        return remote(send2[c].at[e], landing(c, e), s2.at[c, k], r2.at[c, e], (dp, owner(e)))
 
     own2 = [
-        pltpu.make_async_copy(send2.at[h, q], l_rows.at[x, :, strip(h, q)], loc.at[5 + h])
-        for h in range(2)
+        pltpu.make_async_copy(send2[c].at[q], landing(c, q), loc.at[6 + c])
+        for c in range(len(CHUNKS))
     ]
 
-    def reorder(h):
-        loop(CTX - 1, lambda k: first_here(h, k).wait_recv())
-        own1[h].wait()
+    def reorder(c):
+        loop(CTX - 1, lambda k: first_here(c, k).wait_recv())
+        own1[c].wait()
 
         def send(k):
-            pick(h, lax.rem(q + k + 1, 16))
-            second(h, k).start()
+            pick(c, lax.rem(q + k + 1, 16))
+            second(c, k).start()
 
         loop(15, send)
-        pick(h, q)
-        own2[h].start()
-
-    def reordered(h):
-        loop(15, lambda k: second_here(h, k).wait_recv())
-        own2[h].wait()
+        pick(c, q)
+        own2[c].start()
+
+    def reordered(c):
+        loop(15, lambda k: second_here(c, k).wait_recv())
+        own2[c].wait()
 
     to_z = device(x, y, jnp.where(core == 0, up, down), core)
-    mine_w = pl.ds(pl.multiple_of(core * 160, 32), 160)
-    there_w = pl.ds(pl.multiple_of(HID + core * 160, 32), 160)
-    other_w = pl.ds(HID, HID)
-    w_a = [
-        remote(w1.at[mine_w], w1v.at[there_w], wsend.at[0], wrecv.at[0], to_z),
-        remote(bias, bv.at[other_w], wsend.at[1], wrecv.at[1], to_z),
-    ]
-    w_b = [remote(w2.at[mine_w], w2v.at[there_w], wsend.at[2], wrecv.at[2], to_z)]
-    w_c = [remote(w1v.at[there_w], w1v.at[there_w], wsend.at[3], wrecv.at[3], sibling)]
-    w_d = [remote(w2v.at[there_w], w2v.at[there_w], wsend.at[4], wrecv.at[4], sibling)]
+    y_next, y_prev, y_far = lax.rem(y + 1, Y), lax.rem(y + Y - 1, Y), lax.rem(y + 2, Y)
+    w_cols = [pl.ds(pl.multiple_of(core * (n // 2), 128), n // 2) for n in (VIT, LLM)]
+    w_in, w_at = (w1, w2), (w1v, w2v)
+
+    def quarter(r, yy, first_row, count):
+        return w_at[r].at[pl.ds(pl.multiple_of(HID + yy * 80 + first_row, 16), count), w_cols[r]]
+
+    w_z, w_y, w_f, w_c = [], [[], []], [[], []], []
+    for r in range(2):
+        own_quarter = w_in[r].at[pl.ds(pl.multiple_of(y * 80, 16), 80), w_cols[r]]
+        here = quarter(r, y, 0, 80)
+        w_z.append(remote(own_quarter, here, wsend.at[r, 0], wrecv.at[r, 0], to_z))
+        for d, (slot, at) in enumerate(((y_prev, (0, 48)), (y_next, (48, 32)))):
+            w_y[r].append(remote(here, here, wsend.at[r, 1 + d], wrecv.at[r, 1 + d], y_to[d]))
+            piece = quarter(r, slot, *at)
+            w_f[r].append(remote(piece, piece, wsend.at[r, 3 + d], wrecv.at[r, 3 + d], y_to[d]))
+        share = w_at[r].at[pl.ds(HID, HID), w_cols[r]]
+        w_c.append(remote(share, share, wsend.at[r, 5], wrecv.at[r, 5], sibling))
+    w_z.append(remote(bv.at[pl.ds(0, HID)], bv.at[pl.ds(HID, HID)], wsend.at[2, 0], wrecv.at[2, 0], to_z))
+
+    def weights_round(r):
+        w_z[r].wait_recv()
+        start(w_y[r])
+
+    def weights_on(r):
+        received(w_y[r])
+        start(w_f[r])
+
+    def weights_share(r):
+        received(w_f[r])
+        w_c[r].start()
 
     def group(k):
         return pl.ds(k * HID, HID)
 
     def activate(k):
-        pre[group(k)] = dot(w1v[group(k)], n_rows[...].reshape(X * ROWS, VIT), NT)
+        pre[group(k)] = dot(w1v[group(k)], n_rows[0].reshape(X * ROWS, VIT), NT)
 
         def chunk(i):
             at = pl.ds(pl.multiple_of(k * HID + i * 32, 32), 32)
@@ -294,18 +324,20 @@
 
     def hidden(slot, h, k):
         cols = pl.ds(h * HALF, HALF)
-        got = dot(w2v[group(k), cols], l_rows[slot, :, cols], NT)
+        got = dot(w2v[group(k), cols], l_rows[0, slot, :, :, cols].reshape(ROWS, HALF), NT)
         if h == 0:
             hg[group(k), tokens(slot)] = got
         else:
             hg[group(k), tokens(slot)] += got
 
-    def gradient(slot):
+    def pre_grad(slot):
         def chunk(i):
             at = part(i, 64)
             pg[at, tokens(slot)] = (hg[at, tokens(slot)] * pre[at, tokens(slot)]).astype(BF16)
 
         loop(10, chunk)
+
+    def gradient(slot):
         for c in range(2):
             cols = slice(c * 1280, (c + 1) * 1280)
             ng[slot, :, cols] = dot(pg[:, tokens(slot)], w1v[:, cols], TN).astype(BF16)
@@ -313,38 +345,32 @@
     mine = lax.rem(z_lo + core, 2)
     own_h, other_h = (pl.ds(pl.multiple_of(k * HID, HID), HID) for k in (mine, 1 - mine))
 
-    def second_grad(h, at, into):
-        for c in range(4):
-            cols = slice(h * HALF + c * 512, h * HALF + (c + 1) * 512)
-            got = dot(act[at], l_rows[:, :, cols].reshape(X * ROWS, 512), NN).astype(BF16)
-            for i in range(4):
-                into[h, (4 * c + i) % Z, c // 2] = got[:, i * 128 : (i + 1) * 128]
-
-    def first_grad(at, into):
-        for yy in range(Y):
-            got = dot(pg[at], n_rows[:, :, yy * SEG : (yy + 1) * SEG].reshape(X * ROWS, SEG), NN)
-            into[yy] = got.astype(BF16)
-
-    e2 = [remote(g2.at[h], c2.at[h], esend.at[h], erecv.at[h], sibling) for h in range(2)]
-    e1 = remote(g1, c1, esend.at[2], erecv.at[2], sibling)
-
-    def fold2(h):
-        e2[h].wait_recv()
-
-        def add(i):
-            at = (h, i // 2, lax.rem(i, 2))
-            t2[at] = (t2[at].astype(F32) + c2[at].astype(F32)).astype(BF16)
-
-        loop(2 * Z, add)
-
-    def fold1():
-        e1.wait_recv()
-
-        def add(i):
-            at = (i // 5, part(lax.rem(i, 5), 64))
-            t1[at] = (t1[at].astype(F32) + c1[at].astype(F32)).astype(BF16)
-
-        loop(5 * Y, add)
+    def share(src, dst, i):
+        return remote(src, dst, csend.at[i], crecv.at[i], sibling)
+
+    def share_l(h, rows, slots, i):
+        cols = l_cols[h]
+        return share(l_rows.at[0, slots, :, rows, cols], l_rows.at[1, slots, :, rows, cols], i)
+
+    l_cols = [pl.ds(h * HALF, HALF) for h in range(2)]
+    c_n = share(n_rows.at[0], n_rows.at[1], 0)
+    c_act = share(act.at[other_h], act_s, 1)
+    slots = (x, left, right, far)
+    c_pg = [share(pg.at[other_h, tokens(slot)], pg_s.at[:, tokens(slot)], 9 + i) for i, slot in enumerate(slots)]
+    c_l = [share_l(0, slice(0, 64), slice(0, X), 3), share_l(1, slice(0, 32), slice(0, X), 4)]
+    c_last = [share_l(1, slice(32, 64), slot, 5 + i) for i, slot in enumerate(slots)]
+
+    def second_grad(h, c):
+        cols = slice(h * HALF + c * 512, h * HALF + (c + 1) * 512)
+        rows = [l_rows[k, :, :, :, cols].reshape(X * ROWS, 512) for k in range(2)]
+        got = (dot(act[own_h], rows[0], NN) + dot(act_s[...], rows[1], NN)).astype(BF16)
+        for i in range(4):
+            t2[h, (4 * c + i) % Z, c // 2] = got[:, i * 128 : (i + 1) * 128]
+
+    def first_grad(yy):
+        cols = part(yy, SEG)
+        rows = [n_rows[k, :, :, :, cols].reshape(X * ROWS, SEG) for k in range(2)]
+        t1[yy] = (dot(pg[own_h], rows[0], NN) + dot(pg_s[...], rows[1], NN)).astype(BF16)
 
     def keep2(h):
         def finish(own, a, b):
@@ -378,7 +404,7 @@
                 states = vit[at, cols].astype(F32)
                 inv_rms = lax.rsqrt(jnp.mean(states * states, axis=-1, keepdims=True) + EPS)
                 scaled = states * inv_rms
-                g = grad * gain[...]
+                g = grad * gain[...][None, :]
                 out_v[at, cols] = (
                     inv_rms * (g - scaled * jnp.mean(g * scaled, axis=-1, keepdims=True))
                 ).astype(BF16)
@@ -409,84 +435,114 @@
         for r in rings:
             next(r, None)
 
-    l_cols = [pl.ds(h * HALF, HALF) for h in range(2)]
-    l_a = [spread(l_rows, l_cols[h], lsend.at[h], lrecv.at[h]) for h in range(2)]
-    l_f = [forward(l_rows, l_cols[h], lsend.at[h], lrecv.at[h]) for h in range(2)]
-    n_f = forward(n_rows, all_n, nsend, nrecv)
-
+    def l_piece(c):
+        h, rows = CHUNKS[c]
+        return lambda slot, block: l_rows.at[0, slot, block, rows, l_cols[h]]
+
+    l_a = [spread(l_piece(c), lsend.at[c], lrecv.at[c]) for c in range(4)]
+    l_f = [forward(l_piece(c), lsend.at[c], lrecv.at[c]) for c in range(4)]
+
+    start(n_a)
+    offer(0)
+    start(w_z)
     reorder(0)
+    offer(1)
     received(n_a)
     start(n_f)
-    start(w_a)
-    reorder(1)
-    start(w_b)
     reordered(0)
     start(l_a[0])
+    reorder(1)
+    offer(2)
+    weights_round(0)
+    weights_round(1)
     received(n_f)
+    c_n.start()
+    reordered(1)
+    start(l_a[1])
+    received(l_a[0])
+    start(l_f[0])
+    reorder(2)
+    offer(3)
+    weights_on(0)
+    weights_on(1)
     for c in keep_w:
         c.wait()
     activate(0)
-    reordered(1)
-    start(l_a[1])
-    hidden(x, 0, 0)
-    received(l_a[0])
-    start(l_f[0])
-    received(w_a)
-    start(w_c)
-    for slot in (left, right):
-        hidden(slot, 0, 0)
-    hidden(x, 1, 0)
-    received(w_c)
-    activate(1)
     received(l_a[1])
     start(l_f[1])
+    weights_share(0)
+    weights_share(1)
+    reordered(2)
+    start(l_a[2])
+    reorder(3)
+    w_c[0].wait_recv()
+    w_z[2].wait_recv()
+    activate(1)
+    c_act.start()
+    received(l_a[2])
+    start(l_f[2])
     received(l_f[0])
-    second_grad(0, other_h, g2)
-    e2[0].start()
-    second_grad(0, own_h, t2)
-    received(w_b)
-    start(w_d)
-    hidden(far, 0, 0)
-    for slot in (left, right):
-        hidden(slot, 1, 0)
-    fold2(0)
+    received(l_f[1])
+    c_l[0].start()
+    w_c[1].wait_recv()
+    for slot in (x, left):
+        for k in range(2):
+            hidden(slot, 0, k)
+    reordered(3)
+    start(l_a[3])
+    for slot in (right, far):
+        for k in range(2):
+            hidden(slot, 0, k)
+    c_act.wait_recv()
+    c_l[0].wait_recv()
+    c_n.wait_recv()
+    second_grad(0, 0)
+    second_grad(0, 1)
+    received(l_a[3])
+    start(l_f[3])
+    start(c_last[:3])
+    second_grad(0, 2)
+    second_grad(0, 3)
     run(z2_rings[0])
-    received(w_d)
-    for slot in (x, left, right, far):
-        hidden(slot, 0, 1)
-    for slot in (x, left, right):
-        hidden(slot, 1, 1)
-    received(l_f[1])
-    hidden(far, 1, 0)
-    hidden(far, 1, 1)
+    received(l_f[2])
+    c_l[1].start()
+    for i in range(3):
+        for k in range(2):
+            hidden(slots[i], 1, k)
+        pre_grad(slots[i])
+        c_pg[i].start()
+    received(l_f[3])
+    c_last[3].start()
+    for k in range(2):
+        hidden(far, 1, k)
+    pre_grad(far)
+    c_pg[3].start()
     gradient(far)
     run(x_ring)
     run(z2_rings[0])
+    received(c_pg)
+    first_grad(y_far)
+    run(y1_ring)
+    run(z2_rings[0])
+    c_l[1].wait_recv()
+    received(c_last)
+    for c in range(4):
+        second_grad(1, c)
+    run(z2_rings[1])
+    run(z2_rings[0])
     gradient(left)
     gradient(right)
-    gradient(x)
-    first_grad(other_h, g1)
-    e1.start()
-    second_grad(1, other_h, g2)
-    e2[1].start()
     run(x_ring)
-    first_grad(own_h, t1)
-    run(z2_rings[0])
-    second_grad(1, own_h, t2)
-    fold1()
-    run(y1_ring)
-    fold2(1)
     run(z2_rings[1])
-    run(z2_rings[0])
-    run(z2_rings[1])
+    first_grad(y_next)
+    first_grad(y_prev)
     run(y1_ring)
     run(z2_rings[0])
     run(z2_rings[1])
+    first_grad(y)
+    gradient(x)
+    run(z2_rings[1])
     run(y1_ring)
-    run(z1_ring)
-    run(z2_rings[1])
-    run(z1_ring)
-    run(x_ring)
     run(z1_ring)
     run(z2_rings[1])
     run(y2_ring)
@@ -496,30 +552,36 @@
     run(y2_ring)
 
     away = core != z_lo
+    home = [remote(q.at[0], q.at[1], qs.at[i], qr.at[i], swap) for i, q in enumerate((q1, q2))]
+
+    @pl.when(away)
+    def _():
+        q2[0] = f2[...].astype(BF16)
+        home[1].start()
+
+    run(z1_ring)
+    run(x_ring)
+    run(z1_ring)
 
     @pl.when(away)
     def _():
         q1[0] = f1[...].astype(BF16)
-        q2[0] = f2[...].astype(BF16)
-        a = remote(q1.at[0], q1.at[1], qs.at[0], qr.at[0], swap)
-        b = remote(q2.at[0], q2.at[1], qs.at[1], qr.at[1], swap)
-        a.start()
-        b.start()
-        a.wait()
-        b.wait()
+        home[0].start()
+        home[1].wait()
+        out2[...] = q2[1].astype(F32)
+        home[0].wait()
         out1[...] = q1[1].astype(F32)
-        out2[...] = q2[1].astype(F32)
 
     @pl.when(jnp.logical_not(away))
     def _():
         out1[...] = f1[...]
         out2[...] = f2[...]
 
-    for c in n_a + n_f + l_a[0] + l_a[1] + l_f[0] + l_f[1] + w_a + w_b + w_c + w_d + e2 + [e1]:
+    for c in n_a + n_f + sum(l_a + l_f + w_y + w_f, []) + w_z + w_c + c_l + c_last + c_pg + [c_n, c_act]:
         c.wait_send()
-    for h in range(2):
-        loop(CTX - 1, lambda k, h=h: first(h, k).wait_send())
-        loop(15, lambda k, h=h: second(h, k).wait_send())
+    for i in range(4):
+        loop(CTX - 1, lambda k, i=i: first(i, k).wait_send())
+        loop(15, lambda k, i=i: second(i, k).wait_send())
 
 
 def fused(inv, order, frames, llm, vit, gain, bias, w1, w2):
@@ -530,12 +592,12 @@
         return pltpu.VMEM(shape, dtype)
 
     f32 = functools.partial(v, dtype=F32)
-    pairs = [(2, CTX), (2, 16)]
+    pairs = [(4, CTX), (4, 16)]
     sems = []
     for shape in pairs:
         sems += [dma(shape), dma(shape)]
-    sems += [dma((7,))]
-    for shape in ((5,), (4,), (2, 4), (3,), (2, 2), (2, 2), (2, 4), (2, 2, 4), (2, 2), (2,)):
+    sems += [dma((10,))]
+    for shape in ((3, 6), (4,), (4, 4), (13,), (2, 2), (2, 2), (2, 4), (2, 2, 4), (2, 2), (2,)):
         sems += [dma(shape), dma(shape)]
     return pl.pallas_call(
         kernel,
@@ -544,16 +606,16 @@
             jax.ShapeDtypeStruct((80, HID), F32),
             jax.ShapeDtypeStruct((HID, 128), F32),
         ),
-        in_specs=[smem, smem, smem, vmem, vmem, vmem, any_, any_, any_],
+        in_specs=[smem, smem, smem, vmem, vmem, vmem, vmem, any_, any_],
         out_specs=[vmem] * 3,
         scratch_shapes=[
-            v(2, 64, LLM), v(CTX, 64, 128), v(CTX, 64, 128), v(2, 16, ROWS, 128),
-            v(X, ROWS, VIT), v(X, ROWS, LLM),
+            v(2, 64, LLM), *[v(CTX, 32, 128)] * 4, *[v(16, 2, 32, 128)] * 4,
+            v(2, X, 2, 64, VIT), v(2, X, 2, 64, LLM),
             v(2 * HID, VIT), v(2 * HID, LLM), f32(2 * HID, 128),
             f32(2 * HID, X * ROWS), f32(2 * HID, X * ROWS),
             v(2 * HID, X * ROWS), v(2 * HID, X * ROWS), v(X, ROWS, VIT),
-            v(Y, HID, SEG), v(Y, HID, SEG), v(Y, HID, SEG),
-            v(2, Z, 2, HID, 128), v(2, Z, 2, HID, 128), v(2, Z, 2, HID, 128),
+            v(HID, X * ROWS), v(HID, X * ROWS),
+            v(Y, HID, SEG), v(2, Z, 2, HID, 128),
             v(SEG, HID), v(Y, HID, 128), f32(80, HID), f32(HID, 128),
             v(2, 80, HID), v(2, HID, 128),
             v(2, 2, ROWS, VIT), v(2, 1, ROWS, VIT),
@@ -575,7 +637,7 @@
     inverse = jnp.sum(matches * positions[None, :], axis=1)
     vit_grad, first, second = fused(
         inverse, block_order, frame_tokens, llm_grad.reshape(2, 64, LLM), vit_states[0],
-        norm_gain.reshape(1, SEG), jnp.broadcast_to(b_first[:, None], (HID, 128)), w_first, w_second,
+        norm_gain, b_first, w_first, w_second,
     )
     return (vit_grad[None], first.T, second)
 

time: 165 us -> 156 us (0.945)
  Pallas kernels: 154 us -> 149 us
  local copies, waits for them, and re-layouts: 7.84 us -> 5.11 us
    pallas_call x1, Pallas kernels: 154 us -> 149 us  [fused(): pl.pallas_call(kernel, out_shape=(jax.ShapeDtypeStruct((ROWS, VIT), BF16)...]
where the time goes in v3:
time: 156 us
  Pallas kernels  149 us (96%)
  local copies, waits for them, and re-layouts  5.11 us (3%)
    pallas_call x1, Pallas kernels, fused(): pl.pallas_call(kernel, out_shape=(jax.ShapeDtypeStruct((ROWS, VIT), BF16)...  149 us
    unnamed x3, local copies, waits for them, and re-layouts  5.11 us

profile of v3, /device:TPU:1, one launch (start us, length us, event | category | flops | bytes accessed | tf_op | source)
XLA Modules:
  0.0 156.0 jit_solution(15152521649306622214)
XLA Ops:
  0.6 1.3 select_reduce_fusion.inv
  1.9 149.0 %fused.1 = (bf16[128,2560]{1,0:T(8,128)(2,1)}, f32[80,320]{1,0:T(8,128)}, f32[320,128]{1,0:T(8,128)}) custom-call(s32[64]{0:T(128)} %select_reduce_fusion.inv, s32[64]{0:T(128)} %order.1, s32[8,128]{1,0:T(8,128)} %frames.1, bf16[2,64,4096]{2,1,0:T(8,128)(2,1)} %bitcast.4, bf16[128,2560]{1,0:T(8,128)(2,1)} %bitcast.5, f32[640]{0:T(1024)} %gain.1, f32[320]{0:T(512)} %bias.1, ...), custom_call_target="tpu_custom_call" | custom-call | tf_op jit(solution)/shard_map/fused/pallas_call | solution.py:602
  150.9 2.0 %copy.14 = bf16[1,128,2560]{2,1,0:T(8,128)(2,1)} copy(bf16[1,128,2560]{2,1,0:T(8,128)(2,1)} %bitcast.6) | data formatting | bytes 1310720
  152.9 1.6 copy.15
  154.4 1.6 %copy.16 = f32[320,128]{1,0:T(8,128)} copy(f32[320,128]{1,0:T(8,128)} %get-tuple-element.14) | data formatting | bytes 327680

commit v4 on v3

--- a/solution.py
+++ b/solution.py
@@ -444,15 +444,16 @@
 
     start(n_a)
     offer(0)
+    offer(1)
+    reorder(0)
     start(w_z)
-    reorder(0)
-    offer(1)
+    offer(2)
     received(n_a)
     start(n_f)
     reordered(0)
     start(l_a[0])
     reorder(1)
-    offer(2)
+    offer(3)
     weights_round(0)
     weights_round(1)
     received(n_f)
@@ -462,7 +463,6 @@
     received(l_a[0])
     start(l_f[0])
     reorder(2)
-    offer(3)
     weights_on(0)
     weights_on(1)
     for c in keep_w:
@@ -547,6 +547,7 @@
     run(z2_rings[1])
     run(y2_ring)
     run(z1_ring)
+    run(z1_ring)
     run(y2_ring)
     run(z1_ring)
     run(y2_ring)
@@ -560,13 +561,16 @@
         home[1].start()
 
     run(z1_ring)
-    run(x_ring)
-    run(z1_ring)
 
     @pl.when(away)
     def _():
         q1[0] = f1[...].astype(BF16)
         home[0].start()
+
+    run(x_ring)
+
+    @pl.when(away)
+    def _():
         home[1].wait()
         out2[...] = q2[1].astype(F32)
         home[0].wait()

time: 156 us -> 155 us (level)
  no operation moved by 1% of the time
where the time goes in v4:
time: 155 us
  Pallas kernels  148 us (95%)
  local copies, waits for them, and re-layouts  5.11 us (3%)
    pallas_call x1, Pallas kernels, fused(): pl.pallas_call(kernel, out_shape=(jax.ShapeDtypeStruct((ROWS, VIT), BF16)...  148 us
    unnamed x3, local copies, waits for them, and re-layouts  5.11 us

profile of v4, /device:TPU:1, one launch (start us, length us, event | category | flops | bytes accessed | tf_op | source)
XLA Modules:
  0.0 154.7 jit_solution(4725942764123134915)
XLA Ops:
  0.6 1.3 select_reduce_fusion.inv
  1.9 147.7 %fused.1 = (bf16[128,2560]{1,0:T(8,128)(2,1)}, f32[80,320]{1,0:T(8,128)}, f32[320,128]{1,0:T(8,128)}) custom-call(s32[64]{0:T(128)} %select_reduce_fusion.inv, s32[64]{0:T(128)} %order.1, s32[8,128]{1,0:T(8,128)} %frames.1, bf16[2,64,4096]{2,1,0:T(8,128)(2,1)} %bitcast.4, bf16[128,2560]{1,0:T(8,128)(2,1)} %bitcast.5, f32[640]{0:T(1024)} %gain.1, f32[320]{0:T(512)} %bias.1, ...), custom_call_target="tpu_custom_call" | custom-call | tf_op jit(solution)/shard_map/fused/pallas_call | solution.py:606
  149.6 2.0 %copy.14 = bf16[1,128,2560]{2,1,0:T(8,128)(2,1)} copy(bf16[1,128,2560]{2,1,0:T(8,128)(2,1)} %bitcast.6) | data formatting | bytes 1310720
  151.5 1.6 %copy.15 = f32[320,80]{0,1:T(8,128)} copy(f32[320,80]{0,1:T(8,128)} %bitcast.7) | data formatting | bytes 204800
  153.1 1.6 %copy.16 = f32[320,128]{1,0:T(8,128)} copy(f32[320,128]{1,0:T(8,128)} %get-tuple-element.14) | data formatting | bytes 327680

commit v5 on v4

--- a/solution.py
+++ b/solution.py
@@ -529,14 +529,14 @@
     for c in range(4):
         second_grad(1, c)
     run(z2_rings[1])
+    first_grad(y_next)
+    first_grad(y_prev)
+    run(y1_ring)
     run(z2_rings[0])
     gradient(left)
     gradient(right)
     run(x_ring)
     run(z2_rings[1])
-    first_grad(y_next)
-    first_grad(y_prev)
-    run(y1_ring)
     run(z2_rings[0])
     run(z2_rings[1])
     first_grad(y)

time: 155 us -> 156 us (level)
  no operation moved by 1% of the time
where the time goes in v5:
time: 156 us; the launch traced here: 155 us
  Pallas kernels  148 us (95%)
  local copies, waits for them, and re-layouts  5.11 us (3%)
    pallas_call x1, Pallas kernels, fused(): pl.pallas_call(kernel, out_shape=(jax.ShapeDtypeStruct((ROWS, VIT), BF16)...  148 us
    unnamed x3, local copies, waits for them, and re-layouts  5.11 us

profile of v5, /device:TPU:1, one launch (start us, length us, event | category | flops | bytes accessed | tf_op | source)
XLA Modules:
  0.0 155.4 jit_solution(15966461938437987543)
XLA Ops:
  0.6 1.3 select_reduce_fusion.inv
  1.9 148.4 %fused.1 = (bf16[128,2560]{1,0:T(8,128)(2,1)}, f32[80,320]{1,0:T(8,128)}, f32[320,128]{1,0:T(8,128)}) custom-call(s32[64]{0:T(128)} %select_reduce_fusion.inv, s32[64]{0:T(128)} %order.1, s32[8,128]{1,0:T(8,128)} %frames.1, bf16[2,64,4096]{2,1,0:T(8,128)(2,1)} %bitcast.4, bf16[128,2560]{1,0:T(8,128)(2,1)} %bitcast.5, f32[640]{0:T(1024)} %gain.1, f32[320]{0:T(512)} %bias.1, ...), custom_call_target="tpu_custom_call" | custom-call | tf_op jit(solution)/shard_map/fused/pallas_call | solution.py:606
  150.3 2.0 %copy.14 = bf16[1,128,2560]{2,1,0:T(8,128)(2,1)} copy(bf16[1,128,2560]{2,1,0:T(8,128)(2,1)} %bitcast.6) | data formatting | bytes 1310720
  152.3 1.6 %copy.15 = f32[320,80]{0,1:T(8,128)} copy(f32[320,80]{0,1:T(8,128)} %bitcast.7) | data formatting | bytes 204800
  153.8 1.6 %copy.16 = f32[320,128]{1,0:T(8,128)} copy(f32[320,128]{1,0:T(8,128)} %get-tuple-element.14) | data formatting | bytes 327680
